TPU v7x, 128 devices: a whole 4x4x4 slice. The times are simulated.
128 devices in a mesh: wide: 32 (over y, x, z_hi), blk: 4 (over z_lo, core).
Axes of the slice: x: 4, y: 4, z: 4 (z_hi: 2, z_lo: 2; z = z_hi * 2 + z_lo), core: 2. Of those that a mesh axis runs over, the one named last changes fastest.
Arguments:
- visual_features: bfloat16 [131072, 1152], P(('wide', 'blk')), may hold values from -0.1875 to 0.1875
- sentence_features: bfloat16 [4096, 1152], P(('wide', 'blk')), may hold values from -0.1875 to 0.1875
- true_partner_ids: int32 [131072], P(('wide', 'blk')), may hold values from 0 to 4095
- inverse_warmth: float32 [], replicated, may hold values from 90 to 110
- additive_adjust: float32 [], replicated, may hold values from -12 to -9
Outputs:
- grad_images: float32 [131072, 1152], P(('wide', 'blk'))
- grad_texts: float32 [4096, 1152], P(('wide', 'blk'))
Inputs may be any that keep to these rules, and one draw needn't show every extreme that they name: Image i is paired with text true_partner_ids[i]; a text may be paired with several images or none.
All inputs are finite; a program needn't handle non-finite values.
Results may differ from a plain program's by a relative error of at most 0.007.
Values may be sent and summed in bfloat16 or wider, within the bound.
A program may use at most 64 MiB of HBM per device.

v0:
```python
import jax
import jax.numpy as jnp
from jax import lax
from jax.sharding import PartitionSpec as P


def passed_along(array, axis, by):
    peers = lax.axis_size(axis)
    return lax.ppermute(array, axis, [(i, (i + by) % peers) for i in range(peers)])


def remaining_factors(
    visual_features, tile_length, true_partner_ids, leading_offset, inverse_warmth, additive_adjust
):
    cosine_grid = lax.dot_general(
        visual_features, tile_length, (((1,), (1,)), ((), ())), preferred_element_type=jnp.float32
    )
    sigmoid_levels = inverse_warmth * cosine_grid + additive_adjust
    columns = leading_offset + lax.iota(jnp.int32, tile_length.shape[0])
    plus_minus_ones = jnp.where(true_partner_ids[:, None] == columns[None, :], 1.0, -1.0).astype(
        jnp.float32
    )
    return (
        -inverse_warmth * plus_minus_ones * jax.nn.sigmoid(-plus_minus_ones * sigmoid_levels)
    ).astype(jnp.bfloat16)


def both_grads(visual_features, tile_length, loss_grid_scaled):
    incoming_grad_part = jnp.dot(loss_grid_scaled, tile_length, preferred_element_type=jnp.float32)
    returned_grad_part = lax.dot_general(
        loss_grid_scaled,
        visual_features,
        (((0,), (0,)), ((), ())),
        preferred_element_type=jnp.float32,
    )
    return (incoming_grad_part, returned_grad_part)


def shards(visual_features, sentence_features, true_partner_ids, inverse_warmth, additive_adjust):
    width = visual_features.shape[1]
    tdev = sentence_features.shape[0]
    n_wide = lax.axis_size("wide")
    n_blk = lax.axis_size("blk")
    wpos = lax.axis_index("wide")
    caption_group = tdev * n_blk
    held_start = jnp.zeros((tdev, width), jnp.float32)

    def step(turn, carry):
        grad_img, tile_length, held = carry
        reference_offset = (wpos - turn) % n_wide
        joined_tiles = lax.all_gather(tile_length, "blk", axis=0, tiled=True)
        loss_grid_scaled = remaining_factors(
            visual_features,
            joined_tiles,
            true_partner_ids,
            reference_offset * caption_group,
            inverse_warmth,
            additive_adjust,
        )
        incoming_grad_part, returned_grad_part = both_grads(
            visual_features, joined_tiles, loss_grid_scaled
        )
        grad_img = grad_img + incoming_grad_part
        held = held + lax.psum_scatter(
            returned_grad_part.astype(jnp.bfloat16), "blk", scatter_dimension=0, tiled=True
        ).astype(jnp.float32)
        held = passed_along(held, "wide", 1)
        tile_length = passed_along(tile_length, "wide", 1)
        return (grad_img, tile_length, held)

    start = (jnp.zeros(visual_features.shape, jnp.float32), sentence_features, held_start)
    grad_images, span_home, held = lax.fori_loop(0, n_wide, step, start)
    return (grad_images, held)


def solution(mesh):
    return jax.shard_map(
        shards,
        mesh=mesh,
        in_specs=(P(("wide", "blk"), None), P(("wide", "blk"), None), P(("wide", "blk")), P(), P()),
        out_specs=(P(("wide", "blk"), None), P(("wide", "blk"), None)),
        check_vma=False,
    )
```

profile of v0, /device:TPU:0, one launch (start us, length us, event | category | flops | bytes accessed | tf_op | source)
XLA Modules:
  0.0 1250.0 jit_solution(10544662852976132055)
XLA Ops:
  8.7 1234.1 %while.20 = (s32[]{:T(128)}, f32[1024,1152]{1,0:T(8,128)}, bf16[32,1152]{1,0:T(8,128)(2,1)S(1)}, f32[32,1152]{1,0:T(8,128)S(1)}, f32[]{:T(128)}, /*index=5*/s32[...) while((s32[]{:T(128)}, f32[1024,1152]{1,0:T(8,128)}, ...), condition=%wide.region_2.3_spmd.clone, body=%wide.region_0.2_spmd.clone.sunk | while | flops 910123136 | bytes 28145088 | solution.py:72
  8.8 6.6 all_gather.12
  24.2 15.9 %reduce-scatter.2.cloned.1.call-done = bf16[32,1152]{1,0:T(8,128)(2,1)} async-done(((bf16[128,1152]{1,0:T(8,128)(2,1)}), bf16[32,1152]{1,0:T(8,128)(2,1)}) %reduce-scatter.2.cloned.1.call-update) | async-done | bytes 73744 | tf_op jit(solution)/shard_map/while/body/eval_jaxpr/reduce_scatter | solution.py:64
  46.9 6.0 collective-permute-done.1
  53.0 6.0 all_gather.12
  64.2 14.3 %reduce-scatter.2.cloned.1.call-done = bf16[32,1152]{1,0:T(8,128)(2,1)} async-done(((bf16[128,1152]{1,0:T(8,128)(2,1)}), bf16[32,1152]{1,0:T(8,128)(2,1)}) %reduce-scatter.2.cloned.1.call-update) | async-done | bytes 73744 | tf_op jit(solution)/shard_map/while/body/eval_jaxpr/reduce_scatter | solution.py:64
  91.4 6.0 all_gather.12
  102.6 14.3 %reduce-scatter.2.cloned.1.call-done = bf16[32,1152]{1,0:T(8,128)(2,1)} async-done(((bf16[128,1152]{1,0:T(8,128)(2,1)}), bf16[32,1152]{1,0:T(8,128)(2,1)}) %reduce-scatter.2.cloned.1.call-update) | async-done | bytes 73744 | tf_op jit(solution)/shard_map/while/body/eval_jaxpr/reduce_scatter | solution.py:64
  129.7 6.0 all_gather.12
  141.0 14.3 %reduce-scatter.2.cloned.1.call-done = bf16[32,1152]{1,0:T(8,128)(2,1)} async-done(((bf16[128,1152]{1,0:T(8,128)(2,1)}), bf16[32,1152]{1,0:T(8,128)(2,1)}) %reduce-scatter.2.cloned.1.call-update) | async-done | bytes 73744 | tf_op jit(solution)/shard_map/while/body/eval_jaxpr/reduce_scatter | solution.py:64
  168.1 6.0 all_gather.12
  179.4 14.3 %reduce-scatter.2.cloned.1.call-done = bf16[32,1152]{1,0:T(8,128)(2,1)} async-done(((bf16[128,1152]{1,0:T(8,128)(2,1)}), bf16[32,1152]{1,0:T(8,128)(2,1)}) %reduce-scatter.2.cloned.1.call-update) | async-done | bytes 73744 | tf_op jit(solution)/shard_map/while/body/eval_jaxpr/reduce_scatter | solution.py:64
  206.5 6.0 all_gather.12
  217.7 14.3 %reduce-scatter.2.cloned.1.call-done = bf16[32,1152]{1,0:T(8,128)(2,1)} async-done(((bf16[128,1152]{1,0:T(8,128)(2,1)}), bf16[32,1152]{1,0:T(8,128)(2,1)}) %reduce-scatter.2.cloned.1.call-update) | async-done | bytes 73744 | tf_op jit(solution)/shard_map/while/body/eval_jaxpr/reduce_scatter | solution.py:64
  244.9 6.0 all_gather.12
  256.1 14.3 %reduce-scatter.2.cloned.1.call-done = bf16[32,1152]{1,0:T(8,128)(2,1)} async-done(((bf16[128,1152]{1,0:T(8,128)(2,1)}), bf16[32,1152]{1,0:T(8,128)(2,1)}) %reduce-scatter.2.cloned.1.call-update) | async-done | bytes 73744 | tf_op jit(solution)/shard_map/while/body/eval_jaxpr/reduce_scatter | solution.py:64
  283.3 6.0 all_gather.12
  294.5 14.3 %reduce-scatter.2.cloned.1.call-done = bf16[32,1152]{1,0:T(8,128)(2,1)} async-done(((bf16[128,1152]{1,0:T(8,128)(2,1)}), bf16[32,1152]{1,0:T(8,128)(2,1)}) %reduce-scatter.2.cloned.1.call-update) | async-done | bytes 73744 | tf_op jit(solution)/shard_map/while/body/eval_jaxpr/reduce_scatter | solution.py:64
  321.6 6.0 all_gather.12
  332.9 14.3 %reduce-scatter.2.cloned.1.call-done = bf16[32,1152]{1,0:T(8,128)(2,1)} async-done(((bf16[128,1152]{1,0:T(8,128)(2,1)}), bf16[32,1152]{1,0:T(8,128)(2,1)}) %reduce-scatter.2.cloned.1.call-update) | async-done | bytes 73744 | tf_op jit(solution)/shard_map/while/body/eval_jaxpr/reduce_scatter | solution.py:64
  360.0 6.0 all_gather.12
  371.2 14.3 %reduce-scatter.2.cloned.1.call-done = bf16[32,1152]{1,0:T(8,128)(2,1)} async-done(((bf16[128,1152]{1,0:T(8,128)(2,1)}), bf16[32,1152]{1,0:T(8,128)(2,1)}) %reduce-scatter.2.cloned.1.call-update) | async-done | bytes 73744 | tf_op jit(solution)/shard_map/while/body/eval_jaxpr/reduce_scatter | solution.py:64
  398.4 6.0 all_gather.12
  409.6 14.3 %reduce-scatter.2.cloned.1.call-done = bf16[32,1152]{1,0:T(8,128)(2,1)} async-done(((bf16[128,1152]{1,0:T(8,128)(2,1)}), bf16[32,1152]{1,0:T(8,128)(2,1)}) %reduce-scatter.2.cloned.1.call-update) | async-done | bytes 73744 | tf_op jit(solution)/shard_map/while/body/eval_jaxpr/reduce_scatter | solution.py:64
  436.8 6.0 all_gather.12
  448.0 14.3 %reduce-scatter.2.cloned.1.call-done = bf16[32,1152]{1,0:T(8,128)(2,1)} async-done(((bf16[128,1152]{1,0:T(8,128)(2,1)}), bf16[32,1152]{1,0:T(8,128)(2,1)}) %reduce-scatter.2.cloned.1.call-update) | async-done | bytes 73744 | tf_op jit(solution)/shard_map/while/body/eval_jaxpr/reduce_scatter | solution.py:64
  475.2 6.0 all_gather.12
  486.4 14.3 %reduce-scatter.2.cloned.1.call-done = bf16[32,1152]{1,0:T(8,128)(2,1)} async-done(((bf16[128,1152]{1,0:T(8,128)(2,1)}), bf16[32,1152]{1,0:T(8,128)(2,1)}) %reduce-scatter.2.cloned.1.call-update) | async-done | bytes 73744 | tf_op jit(solution)/shard_map/while/body/eval_jaxpr/reduce_scatter | solution.py:64
  513.6 6.0 all_gather.12
  524.8 14.3 %reduce-scatter.2.cloned.1.call-done = bf16[32,1152]{1,0:T(8,128)(2,1)} async-done(((bf16[128,1152]{1,0:T(8,128)(2,1)}), bf16[32,1152]{1,0:T(8,128)(2,1)}) %reduce-scatter.2.cloned.1.call-update) | async-done | bytes 73744 | tf_op jit(solution)/shard_map/while/body/eval_jaxpr/reduce_scatter | solution.py:64
  551.9 6.0 all_gather.12
  563.2 14.3 %reduce-scatter.2.cloned.1.call-done = bf16[32,1152]{1,0:T(8,128)(2,1)} async-done(((bf16[128,1152]{1,0:T(8,128)(2,1)}), bf16[32,1152]{1,0:T(8,128)(2,1)}) %reduce-scatter.2.cloned.1.call-update) | async-done | bytes 73744 | tf_op jit(solution)/shard_map/while/body/eval_jaxpr/reduce_scatter | solution.py:64
  590.3 6.0 all_gather.12
  601.5 14.3 %reduce-scatter.2.cloned.1.call-done = bf16[32,1152]{1,0:T(8,128)(2,1)} async-done(((bf16[128,1152]{1,0:T(8,128)(2,1)}), bf16[32,1152]{1,0:T(8,128)(2,1)}) %reduce-scatter.2.cloned.1.call-update) | async-done | bytes 73744 | tf_op jit(solution)/shard_map/while/body/eval_jaxpr/reduce_scatter | solution.py:64
  628.7 6.0 all_gather.12
  639.9 14.3 %reduce-scatter.2.cloned.1.call-done = bf16[32,1152]{1,0:T(8,128)(2,1)} async-done(((bf16[128,1152]{1,0:T(8,128)(2,1)}), bf16[32,1152]{1,0:T(8,128)(2,1)}) %reduce-scatter.2.cloned.1.call-update) | async-done | bytes 73744 | tf_op jit(solution)/shard_map/while/body/eval_jaxpr/reduce_scatter | solution.py:64
  667.1 6.0 all_gather.12
  678.3 14.3 %reduce-scatter.2.cloned.1.call-done = bf16[32,1152]{1,0:T(8,128)(2,1)} async-done(((bf16[128,1152]{1,0:T(8,128)(2,1)}), bf16[32,1152]{1,0:T(8,128)(2,1)}) %reduce-scatter.2.cloned.1.call-update) | async-done | bytes 73744 | tf_op jit(solution)/shard_map/while/body/eval_jaxpr/reduce_scatter | solution.py:64
  705.5 6.0 all_gather.12
  716.7 14.3 %reduce-scatter.2.cloned.1.call-done = bf16[32,1152]{1,0:T(8,128)(2,1)} async-done(((bf16[128,1152]{1,0:T(8,128)(2,1)}), bf16[32,1152]{1,0:T(8,128)(2,1)}) %reduce-scatter.2.cloned.1.call-update) | async-done | bytes 73744 | tf_op jit(solution)/shard_map/while/body/eval_jaxpr/reduce_scatter | solution.py:64
  743.8 6.0 all_gather.12
  755.1 14.3 %reduce-scatter.2.cloned.1.call-done = bf16[32,1152]{1,0:T(8,128)(2,1)} async-done(((bf16[128,1152]{1,0:T(8,128)(2,1)}), bf16[32,1152]{1,0:T(8,128)(2,1)}) %reduce-scatter.2.cloned.1.call-update) | async-done | bytes 73744 | tf_op jit(solution)/shard_map/while/body/eval_jaxpr/reduce_scatter | solution.py:64
  782.2 6.0 all_gather.12
  793.5 14.3 %reduce-scatter.2.cloned.1.call-done = bf16[32,1152]{1,0:T(8,128)(2,1)} async-done(((bf16[128,1152]{1,0:T(8,128)(2,1)}), bf16[32,1152]{1,0:T(8,128)(2,1)}) %reduce-scatter.2.cloned.1.call-update) | async-done | bytes 73744 | tf_op jit(solution)/shard_map/while/body/eval_jaxpr/reduce_scatter | solution.py:64
  820.6 6.0 all_gather.12
  831.8 14.3 %reduce-scatter.2.cloned.1.call-done = bf16[32,1152]{1,0:T(8,128)(2,1)} async-done(((bf16[128,1152]{1,0:T(8,128)(2,1)}), bf16[32,1152]{1,0:T(8,128)(2,1)}) %reduce-scatter.2.cloned.1.call-update) | async-done | bytes 73744 | tf_op jit(solution)/shard_map/while/body/eval_jaxpr/reduce_scatter | solution.py:64
  859.0 6.0 all_gather.12
  870.2 14.3 %reduce-scatter.2.cloned.1.call-done = bf16[32,1152]{1,0:T(8,128)(2,1)} async-done(((bf16[128,1152]{1,0:T(8,128)(2,1)}), bf16[32,1152]{1,0:T(8,128)(2,1)}) %reduce-scatter.2.cloned.1.call-update) | async-done | bytes 73744 | tf_op jit(solution)/shard_map/while/body/eval_jaxpr/reduce_scatter | solution.py:64
  897.4 6.0 all_gather.12
  908.6 14.3 %reduce-scatter.2.cloned.1.call-done = bf16[32,1152]{1,0:T(8,128)(2,1)} async-done(((bf16[128,1152]{1,0:T(8,128)(2,1)}), bf16[32,1152]{1,0:T(8,128)(2,1)}) %reduce-scatter.2.cloned.1.call-update) | async-done | bytes 73744 | tf_op jit(solution)/shard_map/while/body/eval_jaxpr/reduce_scatter | solution.py:64
  935.8 6.0 all_gather.12
  947.0 14.3 %reduce-scatter.2.cloned.1.call-done = bf16[32,1152]{1,0:T(8,128)(2,1)} async-done(((bf16[128,1152]{1,0:T(8,128)(2,1)}), bf16[32,1152]{1,0:T(8,128)(2,1)}) %reduce-scatter.2.cloned.1.call-update) | async-done | bytes 73744 | tf_op jit(solution)/shard_map/while/body/eval_jaxpr/reduce_scatter | solution.py:64
  974.1 6.0 all_gather.12
  985.4 14.3 %reduce-scatter.2.cloned.1.call-done = bf16[32,1152]{1,0:T(8,128)(2,1)} async-done(((bf16[128,1152]{1,0:T(8,128)(2,1)}), bf16[32,1152]{1,0:T(8,128)(2,1)}) %reduce-scatter.2.cloned.1.call-update) | async-done | bytes 73744 | tf_op jit(solution)/shard_map/while/body/eval_jaxpr/reduce_scatter | solution.py:64
  1012.5 6.0 all_gather.12
  1023.8 14.3 %reduce-scatter.2.cloned.1.call-done = bf16[32,1152]{1,0:T(8,128)(2,1)} async-done(((bf16[128,1152]{1,0:T(8,128)(2,1)}), bf16[32,1152]{1,0:T(8,128)(2,1)}) %reduce-scatter.2.cloned.1.call-update) | async-done | bytes 73744 | tf_op jit(solution)/shard_map/while/body/eval_jaxpr/reduce_scatter | solution.py:64
  1062.1 14.3 %reduce-scatter.2.cloned.1.call-done = bf16[32,1152]{1,0:T(8,128)(2,1)} async-done(((bf16[128,1152]{1,0:T(8,128)(2,1)}), bf16[32,1152]{1,0:T(8,128)(2,1)}) %reduce-scatter.2.cloned.1.call-update) | async-done | bytes 73744 | tf_op jit(solution)/shard_map/while/body/eval_jaxpr/reduce_scatter | solution.py:64
  1100.5 14.3 %reduce-scatter.2.cloned.1.call-done = bf16[32,1152]{1,0:T(8,128)(2,1)} async-done(((bf16[128,1152]{1,0:T(8,128)(2,1)}), bf16[32,1152]{1,0:T(8,128)(2,1)}) %reduce-scatter.2.cloned.1.call-update) | async-done | bytes 73744 | tf_op jit(solution)/shard_map/while/body/eval_jaxpr/reduce_scatter | solution.py:64
  1127.7 6.0 all_gather.12
  1138.9 14.3 %reduce-scatter.2.cloned.1.call-done = bf16[32,1152]{1,0:T(8,128)(2,1)} async-done(((bf16[128,1152]{1,0:T(8,128)(2,1)}), bf16[32,1152]{1,0:T(8,128)(2,1)}) %reduce-scatter.2.cloned.1.call-update) | async-done | bytes 73744 | tf_op jit(solution)/shard_map/while/body/eval_jaxpr/reduce_scatter | solution.py:64
  1166.1 6.0 all_gather.12
  1177.3 14.3 %reduce-scatter.2.cloned.1.call-done = bf16[32,1152]{1,0:T(8,128)(2,1)} async-done(((bf16[128,1152]{1,0:T(8,128)(2,1)}), bf16[32,1152]{1,0:T(8,128)(2,1)}) %reduce-scatter.2.cloned.1.call-update) | async-done | bytes 73744 | tf_op jit(solution)/shard_map/while/body/eval_jaxpr/reduce_scatter | solution.py:64
  1204.4 6.0 all_gather.12
  1215.7 14.3 %reduce-scatter.2.cloned.1.call-done = bf16[32,1152]{1,0:T(8,128)(2,1)} async-done(((bf16[128,1152]{1,0:T(8,128)(2,1)}), bf16[32,1152]{1,0:T(8,128)(2,1)}) %reduce-scatter.2.cloned.1.call-update) | async-done | bytes 73744 | tf_op jit(solution)/shard_map/while/body/eval_jaxpr/reduce_scatter | solution.py:64
  (453 shorter events, 587.7 us)
Async XLA Ops:
  8.8 31.3 %reduce-scatter.2.cloned.1.call-start = ((), (), s32[]{:S(2)}) async-start(), calls=%async_computation.1 | async-start | bytes 368640 | tf_op jit(solution)/shard_map/while/body/eval_jaxpr/reduce_scatter | solution.py:64
  20.5 26.4 %collective-permute-start = (bf16[32,1152]{1,0:T(8,128)(2,1)S(1)}, bf16[32,1152]{1,0:T(8,128)(2,1)S(1)}, u32[]{:S(2)}, u32[]{:S(2)}) collective-permute-start(bf16[32,1152]{1,0:T(8,128)(2,1)S(1)} %copy.13), channel_id=1, source_target_pairs={{0,4},{4,8},{8,12},{12,16},{16,20},{20,24},{24,28},{28,32},{32,36}... | collective-permute-start | bytes 221192 | tf_op jit(solution)/shard_map/while/body/eval_jaxpr/ppermute | solution.py:9
  52.9 25.6 %reduce-scatter.2.cloned.1.call-start = ((), (), s32[]{:S(2)}) async-start(), calls=%async_computation.1 | async-start | bytes 368640 | tf_op jit(solution)/shard_map/while/body/eval_jaxpr/reduce_scatter | solution.py:64
  64.1 24.7 %collective-permute-start = (bf16[32,1152]{1,0:T(8,128)(2,1)S(1)}, bf16[32,1152]{1,0:T(8,128)(2,1)S(1)}, u32[]{:S(2)}, u32[]{:S(2)}) collective-permute-start(bf16[32,1152]{1,0:T(8,128)(2,1)S(1)} %copy.13), channel_id=1, source_target_pairs={{0,4},{4,8},{8,12},{12,16},{16,20},{20,24},{24,28},{28,32},{32,36}... | collective-permute-start | bytes 221192 | tf_op jit(solution)/shard_map/while/body/eval_jaxpr/ppermute | solution.py:9
  91.4 25.5 %reduce-scatter.2.cloned.1.call-start = ((), (), s32[]{:S(2)}) async-start(), calls=%async_computation.1 | async-start | bytes 368640 | tf_op jit(solution)/shard_map/while/body/eval_jaxpr/reduce_scatter | solution.py:64
  102.5 24.7 %collective-permute-start = (bf16[32,1152]{1,0:T(8,128)(2,1)S(1)}, bf16[32,1152]{1,0:T(8,128)(2,1)S(1)}, u32[]{:S(2)}, u32[]{:S(2)}) collective-permute-start(bf16[32,1152]{1,0:T(8,128)(2,1)S(1)} %copy.13), channel_id=1, source_target_pairs={{0,4},{4,8},{8,12},{12,16},{16,20},{20,24},{24,28},{28,32},{32,36}... | collective-permute-start | bytes 221192 | tf_op jit(solution)/shard_map/while/body/eval_jaxpr/ppermute | solution.py:9
  129.7 25.6 %reduce-scatter.2.cloned.1.call-start = ((), (), s32[]{:S(2)}) async-start(), calls=%async_computation.1 | async-start | bytes 368640 | tf_op jit(solution)/shard_map/while/body/eval_jaxpr/reduce_scatter | solution.py:64
  140.9 24.7 %collective-permute-start = (bf16[32,1152]{1,0:T(8,128)(2,1)S(1)}, bf16[32,1152]{1,0:T(8,128)(2,1)S(1)}, u32[]{:S(2)}, u32[]{:S(2)}) collective-permute-start(bf16[32,1152]{1,0:T(8,128)(2,1)S(1)} %copy.13), channel_id=1, source_target_pairs={{0,4},{4,8},{8,12},{12,16},{16,20},{20,24},{24,28},{28,32},{32,36}... | collective-permute-start | bytes 221192 | tf_op jit(solution)/shard_map/while/body/eval_jaxpr/ppermute | solution.py:9
  168.1 25.5 %reduce-scatter.2.cloned.1.call-start = ((), (), s32[]{:S(2)}) async-start(), calls=%async_computation.1 | async-start | bytes 368640 | tf_op jit(solution)/shard_map/while/body/eval_jaxpr/reduce_scatter | solution.py:64
  179.3 24.7 %collective-permute-start = (bf16[32,1152]{1,0:T(8,128)(2,1)S(1)}, bf16[32,1152]{1,0:T(8,128)(2,1)S(1)}, u32[]{:S(2)}, u32[]{:S(2)}) collective-permute-start(bf16[32,1152]{1,0:T(8,128)(2,1)S(1)} %copy.13), channel_id=1, source_target_pairs={{0,4},{4,8},{8,12},{12,16},{16,20},{20,24},{24,28},{28,32},{32,36}... | collective-permute-start | bytes 221192 | tf_op jit(solution)/shard_map/while/body/eval_jaxpr/ppermute | solution.py:9
  206.5 25.6 %reduce-scatter.2.cloned.1.call-start = ((), (), s32[]{:S(2)}) async-start(), calls=%async_computation.1 | async-start | bytes 368640 | tf_op jit(solution)/shard_map/while/body/eval_jaxpr/reduce_scatter | solution.py:64
  217.6 24.7 %collective-permute-start = (bf16[32,1152]{1,0:T(8,128)(2,1)S(1)}, bf16[32,1152]{1,0:T(8,128)(2,1)S(1)}, u32[]{:S(2)}, u32[]{:S(2)}) collective-permute-start(bf16[32,1152]{1,0:T(8,128)(2,1)S(1)} %copy.13), channel_id=1, source_target_pairs={{0,4},{4,8},{8,12},{12,16},{16,20},{20,24},{24,28},{28,32},{32,36}... | collective-permute-start | bytes 221192 | tf_op jit(solution)/shard_map/while/body/eval_jaxpr/ppermute | solution.py:9
  244.8 25.6 %reduce-scatter.2.cloned.1.call-start = ((), (), s32[]{:S(2)}) async-start(), calls=%async_computation.1 | async-start | bytes 368640 | tf_op jit(solution)/shard_map/while/body/eval_jaxpr/reduce_scatter | solution.py:64
  256.0 24.7 %collective-permute-start = (bf16[32,1152]{1,0:T(8,128)(2,1)S(1)}, bf16[32,1152]{1,0:T(8,128)(2,1)S(1)}, u32[]{:S(2)}, u32[]{:S(2)}) collective-permute-start(bf16[32,1152]{1,0:T(8,128)(2,1)S(1)} %copy.13), channel_id=1, source_target_pairs={{0,4},{4,8},{8,12},{12,16},{16,20},{20,24},{24,28},{28,32},{32,36}... | collective-permute-start | bytes 221192 | tf_op jit(solution)/shard_map/while/body/eval_jaxpr/ppermute | solution.py:9
  283.2 25.6 %reduce-scatter.2.cloned.1.call-start = ((), (), s32[]{:S(2)}) async-start(), calls=%async_computation.1 | async-start | bytes 368640 | tf_op jit(solution)/shard_map/while/body/eval_jaxpr/reduce_scatter | solution.py:64
  294.4 24.7 %collective-permute-start = (bf16[32,1152]{1,0:T(8,128)(2,1)S(1)}, bf16[32,1152]{1,0:T(8,128)(2,1)S(1)}, u32[]{:S(2)}, u32[]{:S(2)}) collective-permute-start(bf16[32,1152]{1,0:T(8,128)(2,1)S(1)} %copy.13), channel_id=1, source_target_pairs={{0,4},{4,8},{8,12},{12,16},{16,20},{20,24},{24,28},{28,32},{32,36}... | collective-permute-start | bytes 221192 | tf_op jit(solution)/shard_map/while/body/eval_jaxpr/ppermute | solution.py:9
  321.6 25.6 %reduce-scatter.2.cloned.1.call-start = ((), (), s32[]{:S(2)}) async-start(), calls=%async_computation.1 | async-start | bytes 368640 | tf_op jit(solution)/shard_map/while/body/eval_jaxpr/reduce_scatter | solution.py:64
  332.8 24.7 %collective-permute-start = (bf16[32,1152]{1,0:T(8,128)(2,1)S(1)}, bf16[32,1152]{1,0:T(8,128)(2,1)S(1)}, u32[]{:S(2)}, u32[]{:S(2)}) collective-permute-start(bf16[32,1152]{1,0:T(8,128)(2,1)S(1)} %copy.13), channel_id=1, source_target_pairs={{0,4},{4,8},{8,12},{12,16},{16,20},{20,24},{24,28},{28,32},{32,36}... | collective-permute-start | bytes 221192 | tf_op jit(solution)/shard_map/while/body/eval_jaxpr/ppermute | solution.py:9
  360.0 25.6 %reduce-scatter.2.cloned.1.call-start = ((), (), s32[]{:S(2)}) async-start(), calls=%async_computation.1 | async-start | bytes 368640 | tf_op jit(solution)/shard_map/while/body/eval_jaxpr/reduce_scatter | solution.py:64
  371.2 24.8 %collective-permute-start = (bf16[32,1152]{1,0:T(8,128)(2,1)S(1)}, bf16[32,1152]{1,0:T(8,128)(2,1)S(1)}, u32[]{:S(2)}, u32[]{:S(2)}) collective-permute-start(bf16[32,1152]{1,0:T(8,128)(2,1)S(1)} %copy.13), channel_id=1, source_target_pairs={{0,4},{4,8},{8,12},{12,16},{16,20},{20,24},{24,28},{28,32},{32,36}... | collective-permute-start | bytes 221192 | tf_op jit(solution)/shard_map/while/body/eval_jaxpr/ppermute | solution.py:9
  398.4 25.6 %reduce-scatter.2.cloned.1.call-start = ((), (), s32[]{:S(2)}) async-start(), calls=%async_computation.1 | async-start | bytes 368640 | tf_op jit(solution)/shard_map/while/body/eval_jaxpr/reduce_scatter | solution.py:64
  409.5 24.7 %collective-permute-start = (bf16[32,1152]{1,0:T(8,128)(2,1)S(1)}, bf16[32,1152]{1,0:T(8,128)(2,1)S(1)}, u32[]{:S(2)}, u32[]{:S(2)}) collective-permute-start(bf16[32,1152]{1,0:T(8,128)(2,1)S(1)} %copy.13), channel_id=1, source_target_pairs={{0,4},{4,8},{8,12},{12,16},{16,20},{20,24},{24,28},{28,32},{32,36}... | collective-permute-start | bytes 221192 | tf_op jit(solution)/shard_map/while/body/eval_jaxpr/ppermute | solution.py:9
  436.8 25.6 %reduce-scatter.2.cloned.1.call-start = ((), (), s32[]{:S(2)}) async-start(), calls=%async_computation.1 | async-start | bytes 368640 | tf_op jit(solution)/shard_map/while/body/eval_jaxpr/reduce_scatter | solution.py:64
  447.9 24.7 %collective-permute-start = (bf16[32,1152]{1,0:T(8,128)(2,1)S(1)}, bf16[32,1152]{1,0:T(8,128)(2,1)S(1)}, u32[]{:S(2)}, u32[]{:S(2)}) collective-permute-start(bf16[32,1152]{1,0:T(8,128)(2,1)S(1)} %copy.13), channel_id=1, source_target_pairs={{0,4},{4,8},{8,12},{12,16},{16,20},{20,24},{24,28},{28,32},{32,36}... | collective-permute-start | bytes 221192 | tf_op jit(solution)/shard_map/while/body/eval_jaxpr/ppermute | solution.py:9
  475.1 25.6 %reduce-scatter.2.cloned.1.call-start = ((), (), s32[]{:S(2)}) async-start(), calls=%async_computation.1 | async-start | bytes 368640 | tf_op jit(solution)/shard_map/while/body/eval_jaxpr/reduce_scatter | solution.py:64
  486.3 24.8 %collective-permute-start = (bf16[32,1152]{1,0:T(8,128)(2,1)S(1)}, bf16[32,1152]{1,0:T(8,128)(2,1)S(1)}, u32[]{:S(2)}, u32[]{:S(2)}) collective-permute-start(bf16[32,1152]{1,0:T(8,128)(2,1)S(1)} %copy.13), channel_id=1, source_target_pairs={{0,4},{4,8},{8,12},{12,16},{16,20},{20,24},{24,28},{28,32},{32,36}... | collective-permute-start | bytes 221192 | tf_op jit(solution)/shard_map/while/body/eval_jaxpr/ppermute | solution.py:9
  513.5 25.6 %reduce-scatter.2.cloned.1.call-start = ((), (), s32[]{:S(2)}) async-start(), calls=%async_computation.1 | async-start | bytes 368640 | tf_op jit(solution)/shard_map/while/body/eval_jaxpr/reduce_scatter | solution.py:64
  524.7 24.7 %collective-permute-start = (bf16[32,1152]{1,0:T(8,128)(2,1)S(1)}, bf16[32,1152]{1,0:T(8,128)(2,1)S(1)}, u32[]{:S(2)}, u32[]{:S(2)}) collective-permute-start(bf16[32,1152]{1,0:T(8,128)(2,1)S(1)} %copy.13), channel_id=1, source_target_pairs={{0,4},{4,8},{8,12},{12,16},{16,20},{20,24},{24,28},{28,32},{32,36}... | collective-permute-start | bytes 221192 | tf_op jit(solution)/shard_map/while/body/eval_jaxpr/ppermute | solution.py:9
  551.9 25.6 %reduce-scatter.2.cloned.1.call-start = ((), (), s32[]{:S(2)}) async-start(), calls=%async_computation.1 | async-start | bytes 368640 | tf_op jit(solution)/shard_map/while/body/eval_jaxpr/reduce_scatter | solution.py:64
  563.1 24.8 %collective-permute-start = (bf16[32,1152]{1,0:T(8,128)(2,1)S(1)}, bf16[32,1152]{1,0:T(8,128)(2,1)S(1)}, u32[]{:S(2)}, u32[]{:S(2)}) collective-permute-start(bf16[32,1152]{1,0:T(8,128)(2,1)S(1)} %copy.13), channel_id=1, source_target_pairs={{0,4},{4,8},{8,12},{12,16},{16,20},{20,24},{24,28},{28,32},{32,36}... | collective-permute-start | bytes 221192 | tf_op jit(solution)/shard_map/while/body/eval_jaxpr/ppermute | solution.py:9
  590.3 25.6 %reduce-scatter.2.cloned.1.call-start = ((), (), s32[]{:S(2)}) async-start(), calls=%async_computation.1 | async-start | bytes 368640 | tf_op jit(solution)/shard_map/while/body/eval_jaxpr/reduce_scatter | solution.py:64
  601.5 24.7 %collective-permute-start = (bf16[32,1152]{1,0:T(8,128)(2,1)S(1)}, bf16[32,1152]{1,0:T(8,128)(2,1)S(1)}, u32[]{:S(2)}, u32[]{:S(2)}) collective-permute-start(bf16[32,1152]{1,0:T(8,128)(2,1)S(1)} %copy.13), channel_id=1, source_target_pairs={{0,4},{4,8},{8,12},{12,16},{16,20},{20,24},{24,28},{28,32},{32,36}... | collective-permute-start | bytes 221192 | tf_op jit(solution)/shard_map/while/body/eval_jaxpr/ppermute | solution.py:9
  628.7 25.6 %reduce-scatter.2.cloned.1.call-start = ((), (), s32[]{:S(2)}) async-start(), calls=%async_computation.1 | async-start | bytes 368640 | tf_op jit(solution)/shard_map/while/body/eval_jaxpr/reduce_scatter | solution.py:64
  639.8 24.7 %collective-permute-start = (bf16[32,1152]{1,0:T(8,128)(2,1)S(1)}, bf16[32,1152]{1,0:T(8,128)(2,1)S(1)}, u32[]{:S(2)}, u32[]{:S(2)}) collective-permute-start(bf16[32,1152]{1,0:T(8,128)(2,1)S(1)} %copy.13), channel_id=1, source_target_pairs={{0,4},{4,8},{8,12},{12,16},{16,20},{20,24},{24,28},{28,32},{32,36}... | collective-permute-start | bytes 221192 | tf_op jit(solution)/shard_map/while/body/eval_jaxpr/ppermute | solution.py:9
  667.1 25.6 %reduce-scatter.2.cloned.1.call-start = ((), (), s32[]{:S(2)}) async-start(), calls=%async_computation.1 | async-start | bytes 368640 | tf_op jit(solution)/shard_map/while/body/eval_jaxpr/reduce_scatter | solution.py:64
  678.2 24.7 %collective-permute-start = (bf16[32,1152]{1,0:T(8,128)(2,1)S(1)}, bf16[32,1152]{1,0:T(8,128)(2,1)S(1)}, u32[]{:S(2)}, u32[]{:S(2)}) collective-permute-start(bf16[32,1152]{1,0:T(8,128)(2,1)S(1)} %copy.13), channel_id=1, source_target_pairs={{0,4},{4,8},{8,12},{12,16},{16,20},{20,24},{24,28},{28,32},{32,36}... | collective-permute-start | bytes 221192 | tf_op jit(solution)/shard_map/while/body/eval_jaxpr/ppermute | solution.py:9
  705.4 25.6 %reduce-scatter.2.cloned.1.call-start = ((), (), s32[]{:S(2)}) async-start(), calls=%async_computation.1 | async-start | bytes 368640 | tf_op jit(solution)/shard_map/while/body/eval_jaxpr/reduce_scatter | solution.py:64
  716.6 24.8 %collective-permute-start = (bf16[32,1152]{1,0:T(8,128)(2,1)S(1)}, bf16[32,1152]{1,0:T(8,128)(2,1)S(1)}, u32[]{:S(2)}, u32[]{:S(2)}) collective-permute-start(bf16[32,1152]{1,0:T(8,128)(2,1)S(1)} %copy.13), channel_id=1, source_target_pairs={{0,4},{4,8},{8,12},{12,16},{16,20},{20,24},{24,28},{28,32},{32,36}... | collective-permute-start | bytes 221192 | tf_op jit(solution)/shard_map/while/body/eval_jaxpr/ppermute | solution.py:9
  743.8 25.6 %reduce-scatter.2.cloned.1.call-start = ((), (), s32[]{:S(2)}) async-start(), calls=%async_computation.1 | async-start | bytes 368640 | tf_op jit(solution)/shard_map/while/body/eval_jaxpr/reduce_scatter | solution.py:64
  755.0 24.7 %collective-permute-start = (bf16[32,1152]{1,0:T(8,128)(2,1)S(1)}, bf16[32,1152]{1,0:T(8,128)(2,1)S(1)}, u32[]{:S(2)}, u32[]{:S(2)}) collective-permute-start(bf16[32,1152]{1,0:T(8,128)(2,1)S(1)} %copy.13), channel_id=1, source_target_pairs={{0,4},{4,8},{8,12},{12,16},{16,20},{20,24},{24,28},{28,32},{32,36}... | collective-permute-start | bytes 221192 | tf_op jit(solution)/shard_map/while/body/eval_jaxpr/ppermute | solution.py:9
  782.2 25.6 %reduce-scatter.2.cloned.1.call-start = ((), (), s32[]{:S(2)}) async-start(), calls=%async_computation.1 | async-start | bytes 368640 | tf_op jit(solution)/shard_map/while/body/eval_jaxpr/reduce_scatter | solution.py:64
  793.4 24.7 %collective-permute-start = (bf16[32,1152]{1,0:T(8,128)(2,1)S(1)}, bf16[32,1152]{1,0:T(8,128)(2,1)S(1)}, u32[]{:S(2)}, u32[]{:S(2)}) collective-permute-start(bf16[32,1152]{1,0:T(8,128)(2,1)S(1)} %copy.13), channel_id=1, source_target_pairs={{0,4},{4,8},{8,12},{12,16},{16,20},{20,24},{24,28},{28,32},{32,36}... | collective-permute-start | bytes 221192 | tf_op jit(solution)/shard_map/while/body/eval_jaxpr/ppermute | solution.py:9
  820.6 25.6 %reduce-scatter.2.cloned.1.call-start = ((), (), s32[]{:S(2)}) async-start(), calls=%async_computation.1 | async-start | bytes 368640 | tf_op jit(solution)/shard_map/while/body/eval_jaxpr/reduce_scatter | solution.py:64
  831.8 24.8 %collective-permute-start = (bf16[32,1152]{1,0:T(8,128)(2,1)S(1)}, bf16[32,1152]{1,0:T(8,128)(2,1)S(1)}, u32[]{:S(2)}, u32[]{:S(2)}) collective-permute-start(bf16[32,1152]{1,0:T(8,128)(2,1)S(1)} %copy.13), channel_id=1, source_target_pairs={{0,4},{4,8},{8,12},{12,16},{16,20},{20,24},{24,28},{28,32},{32,36}... | collective-permute-start | bytes 221192 | tf_op jit(solution)/shard_map/while/body/eval_jaxpr/ppermute | solution.py:9
  859.0 25.6 %reduce-scatter.2.cloned.1.call-start = ((), (), s32[]{:S(2)}) async-start(), calls=%async_computation.1 | async-start | bytes 368640 | tf_op jit(solution)/shard_map/while/body/eval_jaxpr/reduce_scatter | solution.py:64
  870.1 24.7 %collective-permute-start = (bf16[32,1152]{1,0:T(8,128)(2,1)S(1)}, bf16[32,1152]{1,0:T(8,128)(2,1)S(1)}, u32[]{:S(2)}, u32[]{:S(2)}) collective-permute-start(bf16[32,1152]{1,0:T(8,128)(2,1)S(1)} %copy.13), channel_id=1, source_target_pairs={{0,4},{4,8},{8,12},{12,16},{16,20},{20,24},{24,28},{28,32},{32,36}... | collective-permute-start | bytes 221192 | tf_op jit(solution)/shard_map/while/body/eval_jaxpr/ppermute | solution.py:9
  897.4 25.6 %reduce-scatter.2.cloned.1.call-start = ((), (), s32[]{:S(2)}) async-start(), calls=%async_computation.1 | async-start | bytes 368640 | tf_op jit(solution)/shard_map/while/body/eval_jaxpr/reduce_scatter | solution.py:64
  908.5 24.7 %collective-permute-start = (bf16[32,1152]{1,0:T(8,128)(2,1)S(1)}, bf16[32,1152]{1,0:T(8,128)(2,1)S(1)}, u32[]{:S(2)}, u32[]{:S(2)}) collective-permute-start(bf16[32,1152]{1,0:T(8,128)(2,1)S(1)} %copy.13), channel_id=1, source_target_pairs={{0,4},{4,8},{8,12},{12,16},{16,20},{20,24},{24,28},{28,32},{32,36}... | collective-permute-start | bytes 221192 | tf_op jit(solution)/shard_map/while/body/eval_jaxpr/ppermute | solution.py:9
  935.7 25.6 %reduce-scatter.2.cloned.1.call-start = ((), (), s32[]{:S(2)}) async-start(), calls=%async_computation.1 | async-start | bytes 368640 | tf_op jit(solution)/shard_map/while/body/eval_jaxpr/reduce_scatter | solution.py:64
  946.9 24.8 %collective-permute-start = (bf16[32,1152]{1,0:T(8,128)(2,1)S(1)}, bf16[32,1152]{1,0:T(8,128)(2,1)S(1)}, u32[]{:S(2)}, u32[]{:S(2)}) collective-permute-start(bf16[32,1152]{1,0:T(8,128)(2,1)S(1)} %copy.13), channel_id=1, source_target_pairs={{0,4},{4,8},{8,12},{12,16},{16,20},{20,24},{24,28},{28,32},{32,36}... | collective-permute-start | bytes 221192 | tf_op jit(solution)/shard_map/while/body/eval_jaxpr/ppermute | solution.py:9
  974.1 25.6 %reduce-scatter.2.cloned.1.call-start = ((), (), s32[]{:S(2)}) async-start(), calls=%async_computation.1 | async-start | bytes 368640 | tf_op jit(solution)/shard_map/while/body/eval_jaxpr/reduce_scatter | solution.py:64
  985.3 24.7 %collective-permute-start = (bf16[32,1152]{1,0:T(8,128)(2,1)S(1)}, bf16[32,1152]{1,0:T(8,128)(2,1)S(1)}, u32[]{:S(2)}, u32[]{:S(2)}) collective-permute-start(bf16[32,1152]{1,0:T(8,128)(2,1)S(1)} %copy.13), channel_id=1, source_target_pairs={{0,4},{4,8},{8,12},{12,16},{16,20},{20,24},{24,28},{28,32},{32,36}... | collective-permute-start | bytes 221192 | tf_op jit(solution)/shard_map/while/body/eval_jaxpr/ppermute | solution.py:9
  1012.5 25.6 %reduce-scatter.2.cloned.1.call-start = ((), (), s32[]{:S(2)}) async-start(), calls=%async_computation.1 | async-start | bytes 368640 | tf_op jit(solution)/shard_map/while/body/eval_jaxpr/reduce_scatter | solution.py:64
  1023.7 24.7 %collective-permute-start = (bf16[32,1152]{1,0:T(8,128)(2,1)S(1)}, bf16[32,1152]{1,0:T(8,128)(2,1)S(1)}, u32[]{:S(2)}, u32[]{:S(2)}) collective-permute-start(bf16[32,1152]{1,0:T(8,128)(2,1)S(1)} %copy.13), channel_id=1, source_target_pairs={{0,4},{4,8},{8,12},{12,16},{16,20},{20,24},{24,28},{28,32},{32,36}... | collective-permute-start | bytes 221192 | tf_op jit(solution)/shard_map/while/body/eval_jaxpr/ppermute | solution.py:9
  1050.9 25.6 %reduce-scatter.2.cloned.1.call-start = ((), (), s32[]{:S(2)}) async-start(), calls=%async_computation.1 | async-start | bytes 368640 | tf_op jit(solution)/shard_map/while/body/eval_jaxpr/reduce_scatter | solution.py:64
  1062.1 24.7 %collective-permute-start = (bf16[32,1152]{1,0:T(8,128)(2,1)S(1)}, bf16[32,1152]{1,0:T(8,128)(2,1)S(1)}, u32[]{:S(2)}, u32[]{:S(2)}) collective-permute-start(bf16[32,1152]{1,0:T(8,128)(2,1)S(1)} %copy.13), channel_id=1, source_target_pairs={{0,4},{4,8},{8,12},{12,16},{16,20},{20,24},{24,28},{28,32},{32,36}... | collective-permute-start | bytes 221192 | tf_op jit(solution)/shard_map/while/body/eval_jaxpr/ppermute | solution.py:9
  1089.3 25.6 %reduce-scatter.2.cloned.1.call-start = ((), (), s32[]{:S(2)}) async-start(), calls=%async_computation.1 | async-start | bytes 368640 | tf_op jit(solution)/shard_map/while/body/eval_jaxpr/reduce_scatter | solution.py:64
  1100.4 24.7 %collective-permute-start = (bf16[32,1152]{1,0:T(8,128)(2,1)S(1)}, bf16[32,1152]{1,0:T(8,128)(2,1)S(1)}, u32[]{:S(2)}, u32[]{:S(2)}) collective-permute-start(bf16[32,1152]{1,0:T(8,128)(2,1)S(1)} %copy.13), channel_id=1, source_target_pairs={{0,4},{4,8},{8,12},{12,16},{16,20},{20,24},{24,28},{28,32},{32,36}... | collective-permute-start | bytes 221192 | tf_op jit(solution)/shard_map/while/body/eval_jaxpr/ppermute | solution.py:9
  1127.7 25.6 %reduce-scatter.2.cloned.1.call-start = ((), (), s32[]{:S(2)}) async-start(), calls=%async_computation.1 | async-start | bytes 368640 | tf_op jit(solution)/shard_map/while/body/eval_jaxpr/reduce_scatter | solution.py:64
  1138.8 24.7 %collective-permute-start = (bf16[32,1152]{1,0:T(8,128)(2,1)S(1)}, bf16[32,1152]{1,0:T(8,128)(2,1)S(1)}, u32[]{:S(2)}, u32[]{:S(2)}) collective-permute-start(bf16[32,1152]{1,0:T(8,128)(2,1)S(1)} %copy.13), channel_id=1, source_target_pairs={{0,4},{4,8},{8,12},{12,16},{16,20},{20,24},{24,28},{28,32},{32,36}... | collective-permute-start | bytes 221192 | tf_op jit(solution)/shard_map/while/body/eval_jaxpr/ppermute | solution.py:9
  1166.0 25.6 %reduce-scatter.2.cloned.1.call-start = ((), (), s32[]{:S(2)}) async-start(), calls=%async_computation.1 | async-start | bytes 368640 | tf_op jit(solution)/shard_map/while/body/eval_jaxpr/reduce_scatter | solution.py:64
  1177.2 24.7 %collective-permute-start = (bf16[32,1152]{1,0:T(8,128)(2,1)S(1)}, bf16[32,1152]{1,0:T(8,128)(2,1)S(1)}, u32[]{:S(2)}, u32[]{:S(2)}) collective-permute-start(bf16[32,1152]{1,0:T(8,128)(2,1)S(1)} %copy.13), channel_id=1, source_target_pairs={{0,4},{4,8},{8,12},{12,16},{16,20},{20,24},{24,28},{28,32},{32,36}... | collective-permute-start | bytes 221192 | tf_op jit(solution)/shard_map/while/body/eval_jaxpr/ppermute | solution.py:9
  1204.4 25.6 %reduce-scatter.2.cloned.1.call-start = ((), (), s32[]{:S(2)}) async-start(), calls=%async_computation.1 | async-start | bytes 368640 | tf_op jit(solution)/shard_map/while/body/eval_jaxpr/reduce_scatter | solution.py:64
  1215.6 24.7 %collective-permute-start = (bf16[32,1152]{1,0:T(8,128)(2,1)S(1)}, bf16[32,1152]{1,0:T(8,128)(2,1)S(1)}, u32[]{:S(2)}, u32[]{:S(2)}) collective-permute-start(bf16[32,1152]{1,0:T(8,128)(2,1)S(1)} %copy.13), channel_id=1, source_target_pairs={{0,4},{4,8},{8,12},{12,16},{16,20},{20,24},{24,28},{28,32},{32,36}... | collective-permute-start | bytes 221192 | tf_op jit(solution)/shard_map/while/body/eval_jaxpr/ppermute | solution.py:9
  (64 other events, 698.3 us)
Sparse Core Ops, SparseCore 0:
  20.7 19.3 reduce-scatter.1
  64.2 14.2 reduce-scatter.1
  102.6 14.1 reduce-scatter.1
  141.0 14.2 reduce-scatter.1
  179.4 14.1 reduce-scatter.1
  217.7 14.2 reduce-scatter.1
  256.1 14.2 reduce-scatter.1
  294.5 14.2 reduce-scatter.1
  332.9 14.2 reduce-scatter.1
  371.3 14.2 reduce-scatter.1
  409.7 14.2 reduce-scatter.1
  448.0 14.2 reduce-scatter.1
  486.4 14.2 reduce-scatter.1
  524.8 14.2 reduce-scatter.1
  563.2 14.2 reduce-scatter.1
  601.6 14.2 reduce-scatter.1
  640.0 14.2 reduce-scatter.1
  678.3 14.2 reduce-scatter.1
  716.7 14.2 reduce-scatter.1
  755.1 14.2 reduce-scatter.1
  793.5 14.2 reduce-scatter.1
  831.9 14.2 reduce-scatter.1
  870.3 14.2 reduce-scatter.1
  908.6 14.2 reduce-scatter.1
  947.0 14.2 reduce-scatter.1
  985.4 14.2 reduce-scatter.1
  1023.8 14.2 reduce-scatter.1
  1062.2 14.2 reduce-scatter.1
  1100.6 14.2 reduce-scatter.1
  1138.9 14.2 reduce-scatter.1
  1177.3 14.2 reduce-scatter.1
  1215.7 14.2 reduce-scatter.1
where the time goes:
time: 1260 us; the launch traced here: 1250 us
  waiting for transfers between devices  543 us (43%)
  matrix products  329 us (26%)
  blocking collectives  193 us (15%)
  starting transfers between devices  138 us (11%)
  other arithmetic  28.9 us (2%)
  between operations  14.4 us (1%)
    reduce_scatter x32, waiting for transfers between devices, step(): lax.psum_scatter(returned_grad_part.astype(jnp.bfloat16), 'blk', scatter_...  459 us
    all_gather x32, blocking collectives, step(): joined_tiles = lax.all_gather(tile_length, 'blk', axis=0, tiled=True)  193 us
    dot_general x32, matrix products, both_grads(): jnp.dot(loss_grid_scaled, tile_length, preferred_element_type=jnp.float32)  167 us
    ppermute x64, starting transfers between devices, passed_along(): lax.ppermute(array, axis, [(i, (i + by) % peers) for i in range(peers)])  138 us
    dot_general x32, matrix products, remaining_factors(): lax.dot_general(visual_features, tile_length, (((1,), (1,)), ((), ())), p...  123 us
    ppermute x64, waiting for transfers between devices, passed_along(): lax.ppermute(array, axis, [(i, (i + by) % peers) for i in range(peers)])  83.1 us
    dot_general x32, matrix products, both_grads(): lax.dot_general(loss_grid_scaled, visual_features, (((0,), (0,)), ((), ()...  40.2 us
    add x32, other arithmetic, step(): held + lax.psum_scatter(returned_grad_part.astype(jnp.bfloat16), 'blk', s...  28.8 us
  transfers between devices with their start and end apart: 96, of which 64 were waited for; matrix products, arithmetic and copies ran while one was open for 16% of the time, Pallas kernels for 0%

commit v1 on v0

v1 whole, which is shorter than its diff:
```python
import jax
import jax.numpy as jnp
from jax import lax
from jax.sharding import PartitionSpec as P

AXES = ("wide", "blk")


def shards(images, texts, partners, scale, bias):
    joined = lax.all_gather(texts, AXES, axis=0, tiled=True)
    scores = lax.dot_general(
        images, joined, (((1,), (1,)), ((), ())), preferred_element_type=jnp.float32
    )
    logits = scale * scores + bias
    columns = lax.iota(jnp.int32, joined.shape[0])
    sign = jnp.where(partners[:, None] == columns[None, :], 1.0, -1.0).astype(jnp.float32)
    weights = (-scale * sign * jax.nn.sigmoid(-sign * logits)).astype(jnp.bfloat16)
    grad_images = jnp.dot(weights, joined, preferred_element_type=jnp.float32)
    part = lax.dot_general(
        weights, images, (((0,), (0,)), ((), ())), preferred_element_type=jnp.float32
    )
    grad_texts = lax.psum_scatter(
        part.astype(jnp.bfloat16), AXES, scatter_dimension=0, tiled=True
    ).astype(jnp.float32)
    return grad_images, grad_texts


def solution(mesh):
    return jax.shard_map(
        shards,
        mesh=mesh,
        in_specs=(P(AXES, None), P(AXES, None), P(AXES), P(), P()),
        out_specs=(P(AXES, None), P(AXES, None)),
        check_vma=False,
    )
```

time: 1260 us -> 343 us (0.27)
  matrix products: 329 us -> 53.3 us
  waiting for transfers between devices: 543 us -> 273 us
  blocking collectives: 193 us -> 0 us
  starting transfers between devices: 138 us -> 0.08 us
  other arithmetic: 28.9 us -> 1.55 us
    dot_general x96 -> x3, matrix products: 329 us -> 53.3 us  [the longest x1 19.9 us: shards(): lax.dot_general(images, joined, (((1,), (1,)), ((), ())), preferred_eleme...]
    reduce_scatter x32 -> x1, waiting for transfers between devices: 459 us -> 197 us  [shards(): lax.psum_scatter(part.astype(jnp.bfloat16), AXES, scatter_dimension=0, ti...]
    all_gather x32 -> x0, blocking collectives: 193 us -> none  [step(): joined_tiles = lax.all_gather(tile_length, 'blk', axis=0, tiled=True)]
    ppermute x64 -> x0, starting transfers between devices: 138 us -> none  [passed_along(): lax.ppermute(array, axis, [(i, (i + by) % peers) for i in range(peers)])]
    ppermute x64 -> x0, waiting for transfers between devices: 83.1 us -> none  [passed_along(): lax.ppermute(array, axis, [(i, (i + by) % peers) for i in range(peers)])]
    all_gather x0 -> x1, waiting for transfers between devices: none -> 75.2 us  [shards(): joined = lax.all_gather(texts, AXES, axis=0, tiled=True)]
    add x64 -> x0, other arithmetic: 28.9 us -> none  [the longest x32 28.8 us: step(): held + lax.psum_scatter(returned_grad_part.astype(jnp.bfloat16), 'blk', s...]
  transfers between devices with their start and end apart: 96 -> 2, of which waited for: 64 -> 2; matrix products, arithmetic and copies ran while one was open for 16% -> 5% of each run, Pallas kernels for 0% -> 0%
where the time goes in v1:
time: 343 us
  waiting for transfers between devices  273 us (80%)
  matrix products  53.3 us (16%)
  between operations  15.3 us (4%)
    reduce_scatter x1, waiting for transfers between devices, shards(): lax.psum_scatter(part.astype(jnp.bfloat16), AXES, scatter_dimension=0, ti...  197 us
    all_gather x1, waiting for transfers between devices, shards(): joined = lax.all_gather(texts, AXES, axis=0, tiled=True)  75.2 us
    dot_general x1, matrix products, shards(): lax.dot_general(images, joined, (((1,), (1,)), ((), ())), preferred_eleme...  19.9 us
    dot_general x1, matrix products, shards(): grad_images = jnp.dot(weights, joined, preferred_element_type=jnp.float32)  17.7 us
    dot_general x1, matrix products, shards(): lax.dot_general(weights, images, (((0,), (0,)), ((), ())), preferred_elem...  15.7 us
  transfers between devices with their start and end apart: 2, of which 2 were waited for; matrix products, arithmetic and copies ran while one was open for 5% of the time, Pallas kernels for 0%

profile of v1, /device:TPU:0, one launch (start us, length us, event | category | flops | bytes accessed | tf_op | source)
XLA Modules:
  0.0 343.1 jit_solution(3602282821613848416)
XLA Ops:
  7.2 0.0 copy-start
  7.2 0.0 all-gather.2.cloned.1.call-start
  7.2 0.7 all-gather.2.cloned.1.call-update
  7.9 0.0 reduce-scatter.2.cloned.1.call-start
  9.3 75.2 %all-gather.2.cloned.1.call-done = bf16[4096,1152]{1,0:T(8,128)(2,1)} async-done(((bf16[32,1152]{1,0:T(8,128)(2,1)}), bf16[4096,1152]{1,0:T(8,128)(2,1)}) %all-gather.2.cloned.1.call-update) | async-done | bytes 9437200 | tf_op jit(solution)/shard_map/all_gather | solution.py:10
  84.4 0.0 copy-done
  84.4 19.9 %fusion.1 = bf16[1024,4096]{1,0:T(8,128)(2,1)} fusion(bf16[1024,1152]{1,0:T(8,128)(2,1)S(1)} %copy-done, bf16[4096,1152]{1,0:T(8,128)(2,1)} %all-gather.2.cloned.1.call-done, f32[]{:T(128)S(6)} %copy.8, f32[]{:T(128)S(6)} %copy.7, s32[1024]{0:T(1024)} %param.7, f32[]{:T(128)S(6)} %neg.9), kind=kOutput, calls=%fused_computation.3 | convolution fusion | flops 9714008064 | bytes 20189196 | tf_op jit(solution)/shard_map/dot_general | solution.py:11
  104.4 15.7 %convolution_convert_fusion = bf16[4096,1152]{1,0:T(8,128)(2,1)} fusion(bf16[1024,4096]{1,0:T(8,128)(2,1)} %fusion.1, bf16[1024,1152]{1,0:T(8,128)(2,1)S(1)} %copy-done), kind=kOutput, calls=%fused_computation.10 | convolution fusion | flops 9668395008 | bytes 20185088 | tf_op jit(solution)/shard_map/dot_general | solution.py:19
  120.0 0.0 reduce-scatter.2.cloned.1.call-update
  120.1 17.7 %fusion.7 = f32[1024,1152]{1,0:T(8,128)} fusion(bf16[1024,4096]{1,0:T(8,128)(2,1)} %fusion.1, bf16[4096,1152]{1,0:T(8,128)(2,1)} %all-gather.2.cloned.1.call-done), kind=kOutput, calls=%fused_computation.11 | convolution fusion | flops 9663676416 | bytes 22544384 | tf_op jit(solution)/shard_map/dot_general | solution.py:18
  137.8 197.0 %reduce-scatter.2.cloned.1.call-done = bf16[32,1152]{1,0:T(8,128)(2,1)} async-done(((bf16[4096,1152]{1,0:T(8,128)(2,1)}), bf16[32,1152]{1,0:T(8,128)(2,1)}) %reduce-scatter.2.cloned.1.call-update) | async-done | bytes 73744 | tf_op jit(solution)/shard_map/reduce_scatter | solution.py:22
  334.7 1.6 convert_element_type.11
Async XLA Ops:
  7.2 77.3 %copy-start = (bf16[1024,1152]{1,0:T(8,128)(2,1)S(1)}, bf16[1024,1152]{1,0:T(8,128)(2,1)}, u32[]{:S(2)}) copy-start(bf16[1024,1152]{1,0:T(8,128)(2,1)} %param.5) | copy-start | bytes 7077892
  7.2 77.2 %all-gather.2.cloned.1.call-start = ((), (), s32[]{:S(2)}) async-start(), calls=%async_computation.1 | async-start | bytes 9510912 | tf_op jit(solution)/shard_map/all_gather | solution.py:10
  7.9 326.8 %reduce-scatter.2.cloned.1.call-start = ((), (), s32[]{:S(2)}) async-start(), calls=%async_computation.2 | async-start | bytes 9510912 | tf_op jit(solution)/shard_map/reduce_scatter | solution.py:22
Sparse Core Ops, SparseCore 0:
  11.0 73.3 all-gather.1
  120.2 214.4 reduce-scatter.1

commit v2 on v1

v2 whole, which is shorter than its diff:
```python
import functools

import jax
import jax.numpy as jnp
from jax import lax
from jax.experimental import pallas as pl
from jax.experimental.pallas import tpu as pltpu
from jax.sharding import PartitionSpec as P

AXES = ("wide", "blk")
MESH = pl.DeviceIdType.MESH
LOG2E = 1.4426950408889634
ORDERS = ((2, 1, 0), (1, 0, 2), (0, 2, 1))
ALL = slice(None)


def here():
    w, b = lax.axis_index("wide"), lax.axis_index("blk")
    return ((w % 2) * 2 + b // 2, w // 8, (w // 2) % 4), b % 2


def device(zyx, core):
    z, y, x = zyx
    return (y * 8 + x * 2 + z // 2, (z % 2) * 2 + core)


def kernel(
    lag,
    scale_ref, bias_ref, ids_ref, images_ref, texts_ref,
    gi_out, gt_out,
    V, T, GI, GT, RB, R1, S1, R2, S2, R3, IDS, IDR, OUT,
    in_sem, v_send, v_recv, id_send, id_recv, gi_send, gi_recv, out_sem,
    a1_send, a1_recv, a2_send, a2_recv, a3_send, a3_recv,
    r1_send, r1_recv, r2_send, r2_recv, r3_send, r3_recv,
):
    me, core = here()
    rows = images_ref.shape[0]
    third = texts_ref.shape[1] // 3
    tdev = texts_ref.shape[0]
    chunk = 8 * tdev
    sibling = device(me, 1 - core)

    def shifted(axis, by):
        pos = list(me)
        pos[axis] = (pos[axis] + by + 4) % 4
        return device(pos, core)

    def part(ref, p, par, half):
        return ref.at[(*par, *half, ALL, pl.ds(p * third, third))]

    def put(axis, offset, seq):
        seq = list(seq)
        seq[axis] = offset
        return tuple(seq)

    own_v = pltpu.make_async_copy(images_ref, V.at[pl.ds(0, rows)], in_sem.at[0])
    own_t = pltpu.make_async_copy(texts_ref, T.at[0, 0, 0, 0, 0, 0], in_sem.at[1])
    own_v.start()
    own_t.start()

    barrier = pltpu.get_barrier_semaphore()
    pl.semaphore_signal(barrier, inc=1, device_id=sibling, device_id_type=MESH)
    for axis in range(3):
        for e in (1, 2, 3):
            pl.semaphore_signal(barrier, inc=1, device_id=shifted(axis, e), device_id_type=MESH)
    pl.semaphore_wait(barrier, 10)

    def remote(src, dst, send, recv, to):
        return pltpu.make_async_remote_copy(
            src_ref=src, dst_ref=dst, send_sem=send, recv_sem=recv, device_id=to, device_id_type=MESH
        )

    own_t.wait()
    light, middle = [], []
    for p, (a1, a2, a3) in enumerate(ORDERS):
        for e in (1, 2, 3):
            zero = (0, 0, 0)
            cp = remote(
                part(T, p, zero, zero),
                part(T, p, put(a1, e % 2, zero), put(a1, e // 2, zero)),
                a1_send.at[p, e - 1], a1_recv.at[p, e - 1], shifted(a1, -e),
            )
            cp.start()
            light.append(cp)

    send_v = remote(images_ref, V.at[pl.ds(rows, rows)], v_send, v_recv, sibling)
    send_v.start()
    send_ids = remote(ids_ref, IDS, id_send, id_recv, sibling)
    send_ids.start()

    for p, (a1, a2, a3) in enumerate(ORDERS):
        for e in (1, 2, 3):
            light[3 * p + e - 1].wait_recv()
        for e in (1, 2, 3):
            along = put(a1, ALL, (0, 0, 0))
            cp = remote(
                part(T, p, along, along),
                part(T, p, put(a2, e % 2, along), put(a2, e // 2, along)),
                a2_send.at[p, e - 1], a2_recv.at[p, e - 1], shifted(a2, -e),
            )
            cp.start()
            middle.append(cp)

    GI[...] = jnp.zeros_like(GI)

    def heavy_gather(p, r, half):
        a3 = ORDERS[p][2]
        e = r[a3] + 2 * half
        both = put(a3, 0, (ALL, ALL, ALL))
        return remote(
            part(T, p, put(a3, 0, r), both),
            part(T, p, r, put(a3, half, both)),
            a3_send.at[p, 4 * r[0] + 2 * r[1] + r[2], half],
            a3_recv.at[p, 4 * r[0] + 2 * r[1] + r[2], half],
            shifted(a3, -e),
        )

    for p in range(3):
        for e in (1, 2, 3):
            middle[3 * p + e - 1].wait_recv()
    for n in range(8):
        r = (n // 4, (n // 2) % 2, n % 2)
        for p in range(3):
            for half in (0, 1):
                if r[ORDERS[p][2]] + 2 * half:
                    heavy_gather(p, r, half).start()

    send_ids.wait_recv()
    for i in range(rows // 128):
        IDR[:, pl.ds(i * 128, 128)] = ids_ref[pl.ds(i, 1), :]
        IDR[:, pl.ds(rows + i * 128, 128)] = IDS[pl.ds(i, 1), :]
    own_v.wait()
    send_v.wait_recv()

    scale = scale_ref[0, 0]
    slope = -scale * LOG2E
    shift = -bias_ref[0, 0] * LOG2E

    def parities(n):
        return (n // 4, (n // 2) % 2, n % 2)

    def heavy_reduce(p, n, half):
        r = parities(n)
        a3 = ORDERS[p][2]
        e = r[a3] + 2 * half
        both = put(a3, half, (ALL, ALL, ALL))
        rest = [r[i] for i in range(3) if i != a3]
        return remote(
            part(GT, p, r, both),
            R1.at[p, e - 1, rest[0], rest[1]],
            r1_send.at[p, n, half], r1_recv.at[p, n, half], shifted(a3, e),
        )

    def middle_reduce(p, q, half):
        a1, a2, a3 = ORDERS[p]
        e = q[a2] + 2 * half
        return remote(
            S1.at[p, q[a2], half, q[a1]],
            R2.at[p, e - 1, q[a1]],
            r2_send.at[p, q[a1], e - 1], r2_recv.at[p, q[a1], e - 1], shifted(a2, e),
        )

    def each_heavy(n, act):
        r = parities(n)
        for p in range(3):
            for half in (0, 1):
                @pl.when(r[ORDERS[p][2]] + 2 * half != 0)
                def _(p=p, half=half):
                    act(p, half)

    def take_in(n):
        r = parities(n)
        each_heavy(n, lambda p, half: heavy_reduce(p, n, half).wait_recv())
        for p, (a1, a2, a3) in enumerate(ORDERS):
            @pl.when(r[a3] == 1)
            def _(p=p, a1=a1, a2=a2, a3=a3):
                rest = [r[i] for i in range(3) if i != a3]
                order = [i for i in range(3) if i != a3]
                own = part(GT, p, put(a3, 0, r), put(a3, 0, (ALL, ALL, ALL)))
                for i in (0, 1):
                    for j in (0, 1):
                        total = own[i, j].astype(jnp.float32)
                        for e in range(3):
                            total += R1[p, e, rest[0], rest[1], i, j].astype(jnp.float32)
                        total = total.astype(jnp.bfloat16)
                        hm, hl = (i, j) if order[0] == a2 else (j, i)
                        S1[p, r[a2], hm, r[a1], hl] = total
                for half in (0, 1):
                    @pl.when(r[a2] + 2 * half != 0)
                    def _(half=half):
                        middle_reduce(p, r, half).start()

    def body(n, _):
        r = parities(n)
        for p in range(3):
            for half in (0, 1):
                @pl.when(r[ORDERS[p][2]] + 2 * half != 0)
                def _(p=p, half=half):
                    heavy_gather(p, r, half).wait_recv()
        tile = T[r[0], r[1], r[2]].reshape(chunk, 3 * third)
        images = V[...]
        scores = lax.dot_general(
            tile, images, (((1,), (1,)), ((), ())), preferred_element_type=jnp.float32
        )
        row = lax.broadcasted_iota(jnp.int32, (chunk, 1), 0)
        at = [
            (me[i] + r[i] + 2 * ((row // (tdev << (2 - i))) % 2)) % 4 for i in range(3)
        ]
        names = (at[1] * 32 + at[2] * 8 + at[0] * 2 + core) * tdev + row % tdev
        match = names == IDR[...]
        t = slope * scores + shift
        t = jnp.where(match, -t, t)
        top = jnp.where(match, -scale, scale)
        weights = (top / (1.0 + jnp.exp2(t))).astype(jnp.bfloat16)
        GT[r[0], r[1], r[2]] = (
            jnp.dot(weights, images, preferred_element_type=jnp.float32)
            .astype(jnp.bfloat16)
            .reshape(2, 2, 2, tdev, 3 * third)
        )
        each_heavy(n, lambda p, half: heavy_reduce(p, n, half).start())
        GI[...] += lax.dot_general(
            weights, tile, (((0,), (0,)), ((), ())), preferred_element_type=jnp.float32
        )

        @pl.when(n >= lag)
        def _():
            take_in(n - lag)

        return 0

    lax.fori_loop(0, 8, body, 0)

    pieces = gi_recv.shape[0]
    step = rows // pieces
    swaps = [
        remote(
            GI.at[pl.ds(rows + i * step, step)], RB.at[pl.ds(i * step, step)],
            gi_send.at[i], gi_recv.at[i], sibling,
        )
        for i in range(pieces)
    ]
    for cp in swaps:
        cp.start()

    def last(n, _):
        take_in(n)
        return 0

    lax.fori_loop(8 - lag, 8, last, 0)

    outs = []

    def finish(i):
        swaps[i].wait_recv()
        at = pl.ds(i * step, step)
        RB[at, :] += GI[at, :]
        cp = pltpu.make_async_copy(RB.at[at], gi_out.at[at], out_sem.at[i])
        cp.start()
        outs.append(cp)

    for i in range(pieces // 2):
        finish(i)
    ends = []
    for p, (a1, a2, a3) in enumerate(ORDERS):
        for par in (0, 1):
            for e in (1, 2, 3):
                pltpu.make_async_copy(
                    R2.at[p, e - 1, par], R2.at[p, e - 1, par], r2_recv.at[p, par, e - 1]
                ).wait()
        for e in (2, 1, 3, 0):
            total = S1[p, 0, 0, e % 2, e // 2].astype(jnp.float32)
            for k in range(3):
                total += R2[p, k, e % 2, e // 2].astype(jnp.float32)
            if e:
                S2[p, e - 1] = total.astype(jnp.bfloat16)
                cp = remote(
                    S2.at[p, e - 1], R3.at[p, e - 1],
                    r3_send.at[p, e - 1], r3_recv.at[p, e - 1], shifted(a1, e),
                )
                cp.start()
                ends.append((p, e, cp))
            else:
                OUT[:, pl.ds(p * third, third)] = total
    for i in range(pieces // 2, pieces):
        finish(i)
    for p, e, cp in ends:
        cp.wait_recv()
    for p in range(3):
        cols = pl.ds(p * third, third)
        total = OUT[:, cols]
        for k in range(3):
            total += R3[p, k].astype(jnp.float32)
        OUT[:, cols] = total
    last_out = pltpu.make_async_copy(OUT, gt_out, out_sem.at[pieces])
    last_out.start()

    for cp in light + middle + [send_v, send_ids] + swaps + [cp for _, _, cp in ends]:
        cp.wait_send()
    for n in range(8):
        r = parities(n)
        for p in range(3):
            for half in (0, 1):
                if r[ORDERS[p][2]] + 2 * half:
                    heavy_gather(p, r, half).wait_send()
                    heavy_reduce(p, n, half).wait_send()
    for p, (a1, a2, a3) in enumerate(ORDERS):
        for low in (0, 1):
            for e in (1, 2, 3):
                q = put(a1, low, put(a2, e % 2, (0, 0, 0)))
                middle_reduce(p, q, e // 2).wait_send()
    for cp in outs + [last_out]:
        cp.wait()


def shards(images, texts, partners, scale, bias):
    rows, width = images.shape
    tdev = texts.shape[0]
    third = width // 3
    vmem = pltpu.VMEM
    sem = pltpu.SemaphoreType.DMA
    pieces = 4
    gathered = (2, 2, 2, 2, 2, 2, tdev, width)
    return pl.pallas_call(
        functools.partial(kernel, 1),
        out_shape=(
            jax.ShapeDtypeStruct((rows, width), jnp.float32),
            jax.ShapeDtypeStruct((tdev, width), jnp.float32),
        ),
        in_specs=[
            pl.BlockSpec(memory_space=pltpu.SMEM),
            pl.BlockSpec(memory_space=pltpu.SMEM),
            pl.BlockSpec(memory_space=pltpu.VMEM),
            pl.BlockSpec(memory_space=pl.ANY),
            pl.BlockSpec(memory_space=pl.ANY),
        ],
        out_specs=(pl.BlockSpec(memory_space=pl.ANY), pl.BlockSpec(memory_space=pl.ANY)),
        scratch_shapes=[
            vmem((2 * rows, width), jnp.bfloat16),
            vmem(gathered, jnp.bfloat16),
            vmem((2 * rows, width), jnp.float32),
            vmem(gathered, jnp.bfloat16),
            vmem((rows, width), jnp.float32),
            vmem((3, 3, 2, 2, 2, 2, tdev, third), jnp.bfloat16),
            vmem((3, 2, 2, 2, 2, tdev, third), jnp.bfloat16),
            vmem((3, 3, 2, 2, tdev, third), jnp.bfloat16),
            vmem((3, 3, tdev, third), jnp.bfloat16),
            vmem((3, 3, tdev, third), jnp.bfloat16),
            vmem((rows // 128, 128), jnp.int32),
            vmem((1, 2 * rows), jnp.int32),
            vmem((tdev, width), jnp.float32),
            sem((2,)), sem, sem, sem, sem, sem((pieces,)), sem((pieces,)), sem((pieces + 1,)),
            sem((3, 3)), sem((3, 3)), sem((3, 3)), sem((3, 3)), sem((3, 8, 2)), sem((3, 8, 2)),
            sem((3, 8, 2)), sem((3, 8, 2)), sem((3, 2, 3)), sem((3, 2, 3)), sem((3, 3)), sem((3, 3)),
        ],
        compiler_params=pltpu.CompilerParams(
            collective_id=0, has_side_effects=True, vmem_limit_bytes=60 * 2**20
        ),
        cost_estimate=pl.CostEstimate(
            flops=3 * 2 * 2 * rows * 64 * tdev * width, bytes_accessed=8 * rows * width, transcendentals=0
        ),
    )(
        scale.reshape(1, 1), bias.reshape(1, 1), partners.reshape(rows // 128, 128), images, texts
    )


def solution(mesh):
    return jax.shard_map(
        shards,
        mesh=mesh,
        in_specs=(P(AXES, None), P(AXES, None), P(AXES), P(), P()),
        out_specs=(P(AXES, None), P(AXES, None)),
        check_vma=False,
    )
```

time: 343 us -> 89.6 us (0.26)
  waiting for transfers between devices: 273 us -> 0 us
  Pallas kernels: 0 us -> 82 us
  matrix products: 53.3 us -> 0 us
  between operations: 15.3 us -> 1.94 us
  local copies, waits for them, and re-layouts: 0.01 us -> 5.53 us
    reduce_scatter x1 -> x0, waiting for transfers between devices: 197 us -> none  [shards(): lax.psum_scatter(part.astype(jnp.bfloat16), AXES, scatter_dimension=0, ti...]
    pallas_call x0 -> x1, Pallas kernels: none -> 82 us  [shards(): pl.pallas_call(functools.partial(kernel, 1), out_shape=(jax.ShapeDtypeStr...]
    all_gather x1 -> x0, waiting for transfers between devices: 75.2 us -> none  [shards(): joined = lax.all_gather(texts, AXES, axis=0, tiled=True)]
    dot_general x3 -> x0, matrix products: 53.3 us -> none  [the longest x1 19.9 us: shards(): lax.dot_general(images, joined, (((1,), (1,)), ((), ())), preferred_eleme...]
    unnamed x2 -> x4, local copies, waits for them, and re-layouts: 0.01 us -> 5.53 us
  transfers between devices with their start and end apart: 2 -> 0, of which waited for: 2 -> 0; matrix products, arithmetic and copies ran while one was open for 5% -> 0% of each run, Pallas kernels for 0% -> 0%
where the time goes in v2:
time: 89.6 us; the launch traced here: 89.4 us
  Pallas kernels  82 us (92%)
  local copies, waits for them, and re-layouts  5.53 us (6%)
  between operations  1.94 us (2%)
    pallas_call x1, Pallas kernels, shards(): pl.pallas_call(functools.partial(kernel, 1), out_shape=(jax.ShapeDtypeStr...  82 us
    unnamed x4, local copies, waits for them, and re-layouts  5.53 us

profile of v2, /device:TPU:0, one launch (start us, length us, event | category | flops | bytes accessed | tf_op | source)
XLA Modules:
  0.0 89.4 jit_solution(621059062693369465)
XLA Ops:
  1.9 82.0 %shard_map.68 = (f32[1024,1152]{1,0:T(8,128)}, f32[32,1152]{1,0:T(8,128)}) custom-call(f32[1,1]{1,0:T(1,128)} %bitcast.3.scale_ref, f32[1,1]{1,0:T(1,128)} %bitcast.4.bias_ref, s32[8,128]{1,0:T(8,128)} %bitcast.5, bf16[1024,1152]{1,0:T(8,128)(2,1)} %images_ref.1, bf16[32,1152]{1,0:T(8,128)(2,1)} %texts_ref.1), custom_call_target="tpu_custom_call" | custom-call | flops 28991029248 | bytes 9437184 | tf_op jit(solution)/shard_map/pallas_call | solution.py:323
  83.9 0.0 copy-start
  83.9 4.9 %copy.11 = f32[1024,1152]{1,0:T(8,128)} copy(f32[1024,1152]{1,0:T(8,128)} %get-tuple-element.4) | data formatting | bytes 9437184
  88.8 0.0 copy-done
  88.8 0.7 copy.12
Async XLA Ops:
  83.9 4.9 %copy-start = (f32[32,1152]{1,0:T(8,128)S(1)}, f32[32,1152]{1,0:T(8,128)}, u32[]{:S(2)}) copy-start(f32[32,1152]{1,0:T(8,128)} %get-tuple-element.5) | copy-start | bytes 442372

commit v3 on v2

--- a/solution.py
+++ b/solution.py
@@ -28,7 +28,7 @@
     lag,
     scale_ref, bias_ref, ids_ref, images_ref, texts_ref,
     gi_out, gt_out,
-    V, T, GI, GT, RB, R1, S1, R2, S2, R3, IDS, IDR, OUT,
+    V, T, W, GI, GT, RB, R1, S1, R2, S2, R3, IDS, IDR, OUT,
     in_sem, v_send, v_recv, id_send, id_recv, gi_send, gi_recv, out_sem,
     a1_send, a1_recv, a2_send, a2_recv, a3_send, a3_recv,
     r1_send, r1_recv, r2_send, r2_recv, r3_send, r3_recv,
@@ -70,60 +70,78 @@
             src_ref=src, dst_ref=dst, send_sem=send, recv_sem=recv, device_id=to, device_id_type=MESH
         )
 
+    def parities(n):
+        m = 7 - n
+        return (m // 4, (m // 2) % 2, m % 2)
+
     own_t.wait()
-    light, middle = [], []
-    for p, (a1, a2, a3) in enumerate(ORDERS):
-        for e in (1, 2, 3):
-            zero = (0, 0, 0)
-            cp = remote(
-                part(T, p, zero, zero),
-                part(T, p, put(a1, e % 2, zero), put(a1, e // 2, zero)),
-                a1_send.at[p, e - 1], a1_recv.at[p, e - 1], shifted(a1, -e),
-            )
-            cp.start()
-            light.append(cp)
-
+    zero = (0, 0, 0)
+
+    def light_gather(p, e):
+        a1 = ORDERS[p][0]
+        return remote(
+            part(T, p, zero, zero),
+            part(T, p, put(a1, e % 2, zero), put(a1, e // 2, zero)),
+            a1_send.at[p, e - 1], a1_recv.at[p, e - 1], shifted(a1, -e),
+        )
+
+    def middle_gather(p, low, e):
+        a1, a2, a3 = ORDERS[p]
+        par, half = put(a1, low, zero), put(a1, ALL, zero)
+        return remote(
+            part(T, p, par, half),
+            part(T, p, put(a2, e % 2, par), put(a2, e // 2, half)),
+            a2_send.at[p, low, e - 1], a2_recv.at[p, low, e - 1], shifted(a2, -e),
+        )
+
+    def heavy_gather(p, n, half):
+        r = parities(n)
+        a3 = ORDERS[p][2]
+        both = put(a3, 0, (ALL, ALL, ALL))
+        return remote(
+            part(T, p, put(a3, 0, r), both),
+            part(T, p, put(a3, 1, r), put(a3, half, both)),
+            a3_send.at[p, n, half], a3_recv.at[p, n, half], shifted(a3, -1 - 2 * half),
+        )
+
+    def pass_on(p, n, half):
+        r = parities(n)
+        a3 = ORDERS[p][2]
+        first = min(i for i in range(3) if i != a3)
+        piece = put(first, half, (ALL, ALL, ALL))
+        return remote(
+            part(T, p, put(a3, 1, r), put(a3, half, piece)),
+            part(T, p, put(a3, 0, r), put(a3, 1, piece)),
+            a3_send.at[p, n, half], a3_recv.at[p, n, half], shifted(a3, 2 * half - 1),
+        )
+
+    for e in (1, 3, 2):
+        for p in range(3):
+            light_gather(p, e).start()
     send_v = remote(images_ref, V.at[pl.ds(rows, rows)], v_send, v_recv, sibling)
     send_v.start()
     send_ids = remote(ids_ref, IDS, id_send, id_recv, sibling)
     send_ids.start()
-
-    for p, (a1, a2, a3) in enumerate(ORDERS):
-        for e in (1, 2, 3):
-            light[3 * p + e - 1].wait_recv()
-        for e in (1, 2, 3):
-            along = put(a1, ALL, (0, 0, 0))
-            cp = remote(
-                part(T, p, along, along),
-                part(T, p, put(a2, e % 2, along), put(a2, e // 2, along)),
-                a2_send.at[p, e - 1], a2_recv.at[p, e - 1], shifted(a2, -e),
-            )
-            cp.start()
-            middle.append(cp)
-
-    GI[...] = jnp.zeros_like(GI)
-
-    def heavy_gather(p, r, half):
-        a3 = ORDERS[p][2]
-        e = r[a3] + 2 * half
-        both = put(a3, 0, (ALL, ALL, ALL))
-        return remote(
-            part(T, p, put(a3, 0, r), both),
-            part(T, p, r, put(a3, half, both)),
-            a3_send.at[p, 4 * r[0] + 2 * r[1] + r[2], half],
-            a3_recv.at[p, 4 * r[0] + 2 * r[1] + r[2], half],
-            shifted(a3, -e),
-        )
-
     for p in range(3):
-        for e in (1, 2, 3):
-            middle[3 * p + e - 1].wait_recv()
+        for e in (1, 3):
+            light_gather(p, e).wait_recv()
+        for e in (1, 3):
+            middle_gather(p, 1, e).start()
+    for p in range(3):
+        light_gather(p, 2).wait_recv()
+        for e in (1, 3):
+            middle_gather(p, 0, e).start()
+    for low in (1, 0):
+        for p in range(3):
+            middle_gather(p, low, 2).start()
     for n in range(8):
-        r = (n // 4, (n // 2) % 2, n % 2)
-        for p in range(3):
-            for half in (0, 1):
-                if r[ORDERS[p][2]] + 2 * half:
-                    heavy_gather(p, r, half).start()
+        r = parities(n)
+        for p, (a1, a2, a3) in enumerate(ORDERS):
+            if r[a3] == 1:
+                for e in (1, 3) if r[a2] else (2,):
+                    middle_gather(p, r[a1], e).wait_recv()
+                for half in (0, 1):
+                    heavy_gather(p, n, half).start()
 
     send_ids.wait_recv()
     for i in range(rows // 128):
@@ -136,9 +154,6 @@
     slope = -scale * LOG2E
     shift = -bias_ref[0, 0] * LOG2E
 
-    def parities(n):
-        return (n // 4, (n // 2) % 2, n % 2)
-
     def heavy_reduce(p, n, half):
         r = parities(n)
         a3 = ORDERS[p][2]
@@ -172,7 +187,7 @@
         r = parities(n)
         each_heavy(n, lambda p, half: heavy_reduce(p, n, half).wait_recv())
         for p, (a1, a2, a3) in enumerate(ORDERS):
-            @pl.when(r[a3] == 1)
+            @pl.when(r[a3] == 0)
             def _(p=p, a1=a1, a2=a2, a3=a3):
                 rest = [r[i] for i in range(3) if i != a3]
                 order = [i for i in range(3) if i != a3]
@@ -190,13 +205,31 @@
                     def _(half=half):
                         middle_reduce(p, r, half).start()
 
+    block = rows // 2
+
+    def image_block(a, i, fresh):
+        at = pl.ds(pl.multiple_of(i * block, block), block)
+        terms = lax.dot_general(
+            W[a, :, at], T[a].reshape(4 * chunk, 3 * third),
+            (((0,), (0,)), ((), ())), preferred_element_type=jnp.float32,
+        )
+        GI[at, :] = terms if fresh else GI[at, :] + terms
+
     def body(n, _):
         r = parities(n)
-        for p in range(3):
-            for half in (0, 1):
-                @pl.when(r[ORDERS[p][2]] + 2 * half != 0)
-                def _(p=p, half=half):
-                    heavy_gather(p, r, half).wait_recv()
+        for p, (a1, a2, a3) in enumerate(ORDERS):
+            @pl.when(r[a3] == 1)
+            def _(p=p, a3=a3):
+                for half in (0, 1):
+                    heavy_gather(p, n, half).wait_recv()
+                for half in (0, 1):
+                    pass_on(p, n + (4 >> a3), half).start()
+
+            @pl.when(r[a3] == 0)
+            def _(p=p):
+                for half in (0, 1):
+                    pass_on(p, n, half).wait_recv()
+
         tile = T[r[0], r[1], r[2]].reshape(chunk, 3 * third)
         images = V[...]
         scores = lax.dot_general(
@@ -218,9 +251,11 @@
             .reshape(2, 2, 2, tdev, 3 * third)
         )
         each_heavy(n, lambda p, half: heavy_reduce(p, n, half).start())
-        GI[...] += lax.dot_general(
-            weights, tile, (((0,), (0,)), ((), ())), preferred_element_type=jnp.float32
-        )
+        W[r[0], pl.ds(pl.multiple_of((2 * r[1] + r[2]) * chunk, chunk), chunk), :] = weights
+
+        @pl.when((n >= 3) & (n < 7))
+        def _():
+            image_block(1, n - 3, True)
 
         @pl.when(n >= lag)
         def _():
@@ -239,14 +274,17 @@
         )
         for i in range(pieces)
     ]
-    for cp in swaps:
-        cp.start()
 
     def last(n, _):
         take_in(n)
         return 0
 
-    lax.fori_loop(8 - lag, 8, last, 0)
+    lax.fori_loop(8 - lag, 7, last, 0)
+    for i in range(pieces):
+        image_block(0, 2 + i, False)
+        swaps[i].start()
+    take_in(7)
+    image_block(0, 0, False)
 
     outs = []
 
@@ -258,8 +296,6 @@
         cp.start()
         outs.append(cp)
 
-    for i in range(pieces // 2):
-        finish(i)
     ends = []
     for p, (a1, a2, a3) in enumerate(ORDERS):
         for par in (0, 1):
@@ -281,7 +317,8 @@
                 ends.append((p, e, cp))
             else:
                 OUT[:, pl.ds(p * third, third)] = total
-    for i in range(pieces // 2, pieces):
+    image_block(0, 1, False)
+    for i in range(pieces):
         finish(i)
     for p, e, cp in ends:
         cp.wait_recv()
@@ -294,14 +331,18 @@
     last_out = pltpu.make_async_copy(OUT, gt_out, out_sem.at[pieces])
     last_out.start()
 
-    for cp in light + middle + [send_v, send_ids] + swaps + [cp for _, _, cp in ends]:
+    for cp in [send_v, send_ids] + swaps + [cp for _, _, cp in ends]:
         cp.wait_send()
-    for n in range(8):
-        r = parities(n)
-        for p in range(3):
+    for p, (a1, a2, a3) in enumerate(ORDERS):
+        for e in (1, 2, 3):
+            light_gather(p, e).wait_send()
+            for low in (0, 1):
+                middle_gather(p, low, e).wait_send()
+        for n in range(8):
+            odd = parities(n)[a3]
             for half in (0, 1):
-                if r[ORDERS[p][2]] + 2 * half:
-                    heavy_gather(p, r, half).wait_send()
+                (heavy_gather if odd else pass_on)(p, n, half).wait_send()
+                if odd + 2 * half:
                     heavy_reduce(p, n, half).wait_send()
     for p, (a1, a2, a3) in enumerate(ORDERS):
         for low in (0, 1):
@@ -318,10 +359,10 @@
     third = width // 3
     vmem = pltpu.VMEM
     sem = pltpu.SemaphoreType.DMA
-    pieces = 4
+    pieces = 2
     gathered = (2, 2, 2, 2, 2, 2, tdev, width)
     return pl.pallas_call(
-        functools.partial(kernel, 1),
+        functools.partial(kernel, 2),
         out_shape=(
             jax.ShapeDtypeStruct((rows, width), jnp.float32),
             jax.ShapeDtypeStruct((tdev, width), jnp.float32),
@@ -337,6 +378,7 @@
         scratch_shapes=[
             vmem((2 * rows, width), jnp.bfloat16),
             vmem(gathered, jnp.bfloat16),
+            vmem((2, 32 * tdev, 2 * rows), jnp.bfloat16),
             vmem((2 * rows, width), jnp.float32),
             vmem(gathered, jnp.bfloat16),
             vmem((rows, width), jnp.float32),
@@ -349,7 +391,7 @@
             vmem((1, 2 * rows), jnp.int32),
             vmem((tdev, width), jnp.float32),
             sem((2,)), sem, sem, sem, sem, sem((pieces,)), sem((pieces,)), sem((pieces + 1,)),
-            sem((3, 3)), sem((3, 3)), sem((3, 3)), sem((3, 3)), sem((3, 8, 2)), sem((3, 8, 2)),
+            sem((3, 3)), sem((3, 3)), sem((3, 2, 3)), sem((3, 2, 3)), sem((3, 8, 2)), sem((3, 8, 2)),
             sem((3, 8, 2)), sem((3, 8, 2)), sem((3, 2, 3)), sem((3, 2, 3)), sem((3, 3)), sem((3, 3)),
         ],
         compiler_params=pltpu.CompilerParams(

time: 89.6 us -> 82.8 us (0.924)
  Pallas kernels: 82 us -> 75.2 us
    pallas_call x1, Pallas kernels: 82 us -> 75.2 us  [shards(): pl.pallas_call(functools.partial(kernel, 2), out_shape=(jax.ShapeDtypeStr...]
where the time goes in v3:
time: 82.8 us; the launch traced here: 82.7 us
  Pallas kernels  75.2 us (91%)
  local copies, waits for them, and re-layouts  5.53 us (7%)
  between operations  1.94 us (2%)
    pallas_call x1, Pallas kernels, shards(): pl.pallas_call(functools.partial(kernel, 2), out_shape=(jax.ShapeDtypeStr...  75.2 us
    unnamed x4, local copies, waits for them, and re-layouts  5.53 us

profile of v3, /device:TPU:0, one launch (start us, length us, event | category | flops | bytes accessed | tf_op | source)
XLA Modules:
  0.0 82.7 jit_solution(11497339566153149817)
XLA Ops:
  1.9 75.2 %shard_map.68 = (f32[1024,1152]{1,0:T(8,128)}, f32[32,1152]{1,0:T(8,128)}) custom-call(f32[1,1]{1,0:T(1,128)} %bitcast.3.scale_ref, f32[1,1]{1,0:T(1,128)} %bitcast.4.bias_ref, s32[8,128]{1,0:T(8,128)} %bitcast.5, bf16[1024,1152]{1,0:T(8,128)(2,1)} %images_ref.1, bf16[32,1152]{1,0:T(8,128)(2,1)} %texts_ref.1), custom_call_target="tpu_custom_call" | custom-call | flops 28991029248 | bytes 9437184 | tf_op jit(solution)/shard_map/pallas_call | solution.py:364
  77.1 0.0 copy-start
  77.1 4.9 %copy.11 = f32[1024,1152]{1,0:T(8,128)} copy(f32[1024,1152]{1,0:T(8,128)} %get-tuple-element.4) | data formatting | bytes 9437184
  82.0 0.0 copy-done
  82.0 0.7 copy.12
Async XLA Ops:
  77.1 4.9 %copy-start = (f32[32,1152]{1,0:T(8,128)S(1)}, f32[32,1152]{1,0:T(8,128)}, u32[]{:S(2)}) copy-start(f32[32,1152]{1,0:T(8,128)} %get-tuple-element.5) | copy-start | bytes 442372

commit v4 on v3

--- a/solution.py
+++ b/solution.py
@@ -12,6 +12,7 @@
 LOG2E = 1.4426950408889634
 ORDERS = ((2, 1, 0), (1, 0, 2), (0, 2, 1))
 ALL = slice(None)
+AHEAD = 2
 
 
 def here():
@@ -28,8 +29,8 @@
     lag,
     scale_ref, bias_ref, ids_ref, images_ref, texts_ref,
     gi_out, gt_out,
-    V, T, W, GI, GT, RB, R1, S1, R2, S2, R3, IDS, IDR, OUT,
-    in_sem, v_send, v_recv, id_send, id_recv, gi_send, gi_recv, out_sem,
+    V, T, W, GI, GT, RB, R1, S1, R2, S2, R3, IDS, IDR,
+    in_sem, v_send, v_recv, id_send, id_recv, gi_send, gi_recv,
     a1_send, a1_recv, a2_send, a2_recv, a3_send, a3_recv,
     r1_send, r1_recv, r2_send, r2_recv, r3_send, r3_recv,
 ):
@@ -134,14 +135,21 @@
     for low in (1, 0):
         for p in range(3):
             middle_gather(p, low, 2).start()
-    for n in range(8):
+    waited = set()
+    for n in range(AHEAD):
         r = parities(n)
         for p, (a1, a2, a3) in enumerate(ORDERS):
             if r[a3] == 1:
                 for e in (1, 3) if r[a2] else (2,):
+                    waited.add((p, r[a1], e))
                     middle_gather(p, r[a1], e).wait_recv()
                 for half in (0, 1):
                     heavy_gather(p, n, half).start()
+    for p in range(3):
+        for low in (1, 0):
+            for e in (1, 3, 2):
+                if (p, low, e) not in waited:
+                    middle_gather(p, low, e).wait_recv()
 
     send_ids.wait_recv()
     for i in range(rows // 128):
@@ -205,15 +213,15 @@
                     def _(half=half):
                         middle_reduce(p, r, half).start()
 
-    block = rows // 2
-
-    def image_block(a, i, fresh):
-        at = pl.ds(pl.multiple_of(i * block, block), block)
-        terms = lax.dot_general(
-            W[a, :, at], T[a].reshape(4 * chunk, 3 * third),
+    pieces = gi_recv.shape[0]
+    block = rows // pieces
+
+    def image_block(i):
+        at = pl.ds(i * block, block)
+        GI[at, :] = lax.dot_general(
+            W[:, at], T[...].reshape(8 * chunk, 3 * third),
             (((0,), (0,)), ((), ())), preferred_element_type=jnp.float32,
         )
-        GI[at, :] = terms if fresh else GI[at, :] + terms
 
     def body(n, _):
         r = parities(n)
@@ -229,6 +237,13 @@
             def _(p=p):
                 for half in (0, 1):
                     pass_on(p, n, half).wait_recv()
+
+        ahead = parities(n + AHEAD)
+        for p, (a1, a2, a3) in enumerate(ORDERS):
+            @pl.when((n + AHEAD < 8) & (ahead[a3] == 1))
+            def _(p=p):
+                for half in (0, 1):
+                    heavy_gather(p, n + AHEAD, half).start()
 
         tile = T[r[0], r[1], r[2]].reshape(chunk, 3 * third)
         images = V[...]
@@ -251,11 +266,7 @@
             .reshape(2, 2, 2, tdev, 3 * third)
         )
         each_heavy(n, lambda p, half: heavy_reduce(p, n, half).start())
-        W[r[0], pl.ds(pl.multiple_of((2 * r[1] + r[2]) * chunk, chunk), chunk), :] = weights
-
-        @pl.when((n >= 3) & (n < 7))
-        def _():
-            image_block(1, n - 3, True)
+        W[pl.ds(pl.multiple_of((7 - n) * chunk, chunk), chunk), :] = weights
 
         @pl.when(n >= lag)
         def _():
@@ -265,8 +276,7 @@
 
     lax.fori_loop(0, 8, body, 0)
 
-    pieces = gi_recv.shape[0]
-    step = rows // pieces
+    step = block
     swaps = [
         remote(
             GI.at[pl.ds(rows + i * step, step)], RB.at[pl.ds(i * step, step)],
@@ -275,27 +285,18 @@
         for i in range(pieces)
     ]
 
-    def last(n, _):
-        take_in(n)
-        return 0
-
-    lax.fori_loop(8 - lag, 7, last, 0)
-    for i in range(pieces):
-        image_block(0, 2 + i, False)
-        swaps[i].start()
-    take_in(7)
-    image_block(0, 0, False)
-
-    outs = []
-
     def finish(i):
         swaps[i].wait_recv()
         at = pl.ds(i * step, step)
-        RB[at, :] += GI[at, :]
-        cp = pltpu.make_async_copy(RB.at[at], gi_out.at[at], out_sem.at[i])
-        cp.start()
-        outs.append(cp)
-
+        gi_out[at, :] = RB[at, :] + GI[at, :]
+
+    for i in range(pieces):
+        image_block(pieces + i)
+        swaps[i].start()
+        if i in (0, 2):
+            take_in(6 + i // 2)
+    for i in range(2):
+        image_block(i)
     ends = []
     for p, (a1, a2, a3) in enumerate(ORDERS):
         for par in (0, 1):
@@ -316,20 +317,20 @@
                 cp.start()
                 ends.append((p, e, cp))
             else:
-                OUT[:, pl.ds(p * third, third)] = total
-    image_block(0, 1, False)
-    for i in range(pieces):
+                gt_out[:, pl.ds(p * third, third)] = total
+    for i in range(2):
+        finish(i)
+    for i in range(2, pieces):
+        image_block(i)
         finish(i)
     for p, e, cp in ends:
         cp.wait_recv()
     for p in range(3):
         cols = pl.ds(p * third, third)
-        total = OUT[:, cols]
+        total = gt_out[:, cols]
         for k in range(3):
             total += R3[p, k].astype(jnp.float32)
-        OUT[:, cols] = total
-    last_out = pltpu.make_async_copy(OUT, gt_out, out_sem.at[pieces])
-    last_out.start()
+        gt_out[:, cols] = total
 
     for cp in [send_v, send_ids] + swaps + [cp for _, _, cp in ends]:
         cp.wait_send()
@@ -349,8 +350,6 @@
             for e in (1, 2, 3):
                 q = put(a1, low, put(a2, e % 2, (0, 0, 0)))
                 middle_reduce(p, q, e // 2).wait_send()
-    for cp in outs + [last_out]:
-        cp.wait()
 
 
 def shards(images, texts, partners, scale, bias):
@@ -359,26 +358,26 @@
     third = width // 3
     vmem = pltpu.VMEM
     sem = pltpu.SemaphoreType.DMA
-    pieces = 2
+    pieces = 4
     gathered = (2, 2, 2, 2, 2, 2, tdev, width)
     return pl.pallas_call(
         functools.partial(kernel, 2),
         out_shape=(
-            jax.ShapeDtypeStruct((rows, width), jnp.float32),
-            jax.ShapeDtypeStruct((tdev, width), jnp.float32),
+            pltpu.VMEM((rows, width), jnp.float32),
+            pltpu.VMEM((tdev, width), jnp.float32),
         ),
         in_specs=[
             pl.BlockSpec(memory_space=pltpu.SMEM),
             pl.BlockSpec(memory_space=pltpu.SMEM),
             pl.BlockSpec(memory_space=pltpu.VMEM),
-            pl.BlockSpec(memory_space=pl.ANY),
-            pl.BlockSpec(memory_space=pl.ANY),
+            pl.BlockSpec(memory_space=pltpu.HBM),
+            pl.BlockSpec(memory_space=pltpu.HBM),
         ],
-        out_specs=(pl.BlockSpec(memory_space=pl.ANY), pl.BlockSpec(memory_space=pl.ANY)),
+        out_specs=(pl.BlockSpec(memory_space=pltpu.VMEM), pl.BlockSpec(memory_space=pltpu.VMEM)),
         scratch_shapes=[
             vmem((2 * rows, width), jnp.bfloat16),
             vmem(gathered, jnp.bfloat16),
-            vmem((2, 32 * tdev, 2 * rows), jnp.bfloat16),
+            vmem((64 * tdev, 2 * rows), jnp.bfloat16),
             vmem((2 * rows, width), jnp.float32),
             vmem(gathered, jnp.bfloat16),
             vmem((rows, width), jnp.float32),
@@ -389,13 +388,12 @@
             vmem((3, 3, tdev, third), jnp.bfloat16),
             vmem((rows // 128, 128), jnp.int32),
             vmem((1, 2 * rows), jnp.int32),
-            vmem((tdev, width), jnp.float32),
-            sem((2,)), sem, sem, sem, sem, sem((pieces,)), sem((pieces,)), sem((pieces + 1,)),
+            sem((2,)), sem, sem, sem, sem, sem((pieces,)), sem((pieces,)),
             sem((3, 3)), sem((3, 3)), sem((3, 2, 3)), sem((3, 2, 3)), sem((3, 8, 2)), sem((3, 8, 2)),
             sem((3, 8, 2)), sem((3, 8, 2)), sem((3, 2, 3)), sem((3, 2, 3)), sem((3, 3)), sem((3, 3)),
         ],
         compiler_params=pltpu.CompilerParams(
-            collective_id=0, has_side_effects=True, vmem_limit_bytes=60 * 2**20
+            collective_id=0, has_side_effects=True, vmem_limit_bytes=52 * 2**20
         ),
         cost_estimate=pl.CostEstimate(
             flops=3 * 2 * 2 * rows * 64 * tdev * width, bytes_accessed=8 * rows * width, transcendentals=0

time: 82.8 us -> 74.2 us (0.90)
  Pallas kernels: 75.2 us -> 69.2 us
  local copies, waits for them, and re-layouts: 5.53 us -> 2.85 us
    pallas_call x1, Pallas kernels: 75.2 us -> 69.2 us  [shards(): pl.pallas_call(functools.partial(kernel, 2), out_shape=(pltpu.VMEM((rows,...]
    unnamed x4 -> x2, local copies, waits for them, and re-layouts: 5.53 us -> 2.85 us
where the time goes in v4:
time: 74.2 us; the launch traced here: 74 us
  Pallas kernels  69.2 us (93%)
  local copies, waits for them, and re-layouts  2.85 us (4%)
  between operations  1.93 us (3%)
    pallas_call x1, Pallas kernels, shards(): pl.pallas_call(functools.partial(kernel, 2), out_shape=(pltpu.VMEM((rows,...  69.2 us
    unnamed x2, local copies, waits for them, and re-layouts  2.85 us

profile of v4, /device:TPU:0, one launch (start us, length us, event | category | flops | bytes accessed | tf_op | source)
XLA Modules:
  0.0 74.0 jit_solution(3340248911565156743)
XLA Ops:
  1.9 69.2 %shard_map.68 = (f32[1024,1152]{1,0:T(8,128)S(1)}, f32[32,1152]{1,0:T(8,128)S(1)}) custom-call(f32[1,1]{1,0:T(1,128)} %bitcast.3.scale_ref, f32[1,1]{1,0:T(1,128)} %bitcast.4.bias_ref, s32[8,128]{1,0:T(8,128)} %bitcast.5, bf16[1024,1152]{1,0:T(8,128)(2,1)} %images_ref.1, bf16[32,1152]{1,0:T(8,128)(2,1)} %texts_ref.1), custom_call_target="tpu_custom_call" | custom-call | flops 28991029248 | bytes 9437184 | tf_op jit(solution)/shard_map/pallas_call | solution.py:363
  71.2 2.2 %copy.9 = f32[1024,1152]{1,0:T(8,128)} copy(f32[1024,1152]{1,0:T(8,128)S(1)} %get-tuple-element.2) | data formatting | bytes 9437184
  73.4 0.7 copy.10

commit v5 on v4

--- a/solution.py
+++ b/solution.py
@@ -293,31 +293,35 @@
     for i in range(pieces):
         image_block(pieces + i)
         swaps[i].start()
-        if i in (0, 2):
-            take_in(6 + i // 2)
-    for i in range(2):
-        image_block(i)
+        if i < 3:
+            take_in(5 + i)
     ends = []
-    for p, (a1, a2, a3) in enumerate(ORDERS):
-        for par in (0, 1):
+
+    def light_reduce(par):
+        for p, (a1, a2, a3) in enumerate(ORDERS):
             for e in (1, 2, 3):
                 pltpu.make_async_copy(
                     R2.at[p, e - 1, par], R2.at[p, e - 1, par], r2_recv.at[p, par, e - 1]
                 ).wait()
-        for e in (2, 1, 3, 0):
-            total = S1[p, 0, 0, e % 2, e // 2].astype(jnp.float32)
-            for k in range(3):
-                total += R2[p, k, e % 2, e // 2].astype(jnp.float32)
-            if e:
-                S2[p, e - 1] = total.astype(jnp.bfloat16)
-                cp = remote(
-                    S2.at[p, e - 1], R3.at[p, e - 1],
-                    r3_send.at[p, e - 1], r3_recv.at[p, e - 1], shifted(a1, e),
-                )
-                cp.start()
-                ends.append((p, e, cp))
-            else:
-                gt_out[:, pl.ds(p * third, third)] = total
+            for e in (1, 3) if par else (2, 0):
+                total = S1[p, 0, 0, e % 2, e // 2].astype(jnp.float32)
+                for k in range(3):
+                    total += R2[p, k, e % 2, e // 2].astype(jnp.float32)
+                if e:
+                    S2[p, e - 1] = total.astype(jnp.bfloat16)
+                    cp = remote(
+                        S2.at[p, e - 1], R3.at[p, e - 1],
+                        r3_send.at[p, e - 1], r3_recv.at[p, e - 1], shifted(a1, e),
+                    )
+                    cp.start()
+                    ends.append((p, e, cp))
+                else:
+                    gt_out[:, pl.ds(p * third, third)] = total
+
+    image_block(0)
+    light_reduce(1)
+    image_block(1)
+    light_reduce(0)
     for i in range(2):
         finish(i)
     for i in range(2, pieces):
@@ -361,7 +365,7 @@
     pieces = 4
     gathered = (2, 2, 2, 2, 2, 2, tdev, width)
     return pl.pallas_call(
-        functools.partial(kernel, 2),
+        functools.partial(kernel, 3),
         out_shape=(
             pltpu.VMEM((rows, width), jnp.float32),
             pltpu.VMEM((tdev, width), jnp.float32),

time: 74.2 us -> 74.4 us (level)
  no operation moved by 1% of the time
where the time goes in v5:
time: 74.4 us; the launch traced here: 74.2 us
  Pallas kernels  69.5 us (93%)
  local copies, waits for them, and re-layouts  2.85 us (4%)
  between operations  1.93 us (3%)
    pallas_call x1, Pallas kernels, shards(): pl.pallas_call(functools.partial(kernel, 3), out_shape=(pltpu.VMEM((rows,...  69.5 us
    unnamed x2, local copies, waits for them, and re-layouts  2.85 us

profile of v5, /device:TPU:0, one launch (start us, length us, event | category | flops | bytes accessed | tf_op | source)
XLA Modules:
  0.0 74.2 jit_solution(10668143000321650919)
XLA Ops:
  1.9 69.5 %shard_map.68 = (f32[1024,1152]{1,0:T(8,128)S(1)}, f32[32,1152]{1,0:T(8,128)S(1)}) custom-call(f32[1,1]{1,0:T(1,128)} %bitcast.3.scale_ref, f32[1,1]{1,0:T(1,128)} %bitcast.4.bias_ref, s32[8,128]{1,0:T(8,128)} %bitcast.5, bf16[1024,1152]{1,0:T(8,128)(2,1)} %images_ref.1, bf16[32,1152]{1,0:T(8,128)(2,1)} %texts_ref.1), custom_call_target="tpu_custom_call" | custom-call | flops 28991029248 | bytes 9437184 | tf_op jit(solution)/shard_map/pallas_call | solution.py:367
  71.4 2.2 %copy.9 = f32[1024,1152]{1,0:T(8,128)} copy(f32[1024,1152]{1,0:T(8,128)S(1)} %get-tuple-element.2) | data formatting | bytes 9437184
  73.6 0.7 copy.10

commit v6 on v4

--- a/solution.py
+++ b/solution.py
@@ -216,8 +216,8 @@
     pieces = gi_recv.shape[0]
     block = rows // pieces
 
-    def image_block(i):
-        at = pl.ds(i * block, block)
+    def image_block(i, count=1):
+        at = pl.ds(i * block, count * block)
         GI[at, :] = lax.dot_general(
             W[:, at], T[...].reshape(8 * chunk, 3 * third),
             (((0,), (0,)), ((), ())), preferred_element_type=jnp.float32,
@@ -295,8 +295,7 @@
         swaps[i].start()
         if i in (0, 2):
             take_in(6 + i // 2)
-    for i in range(2):
-        image_block(i)
+    image_block(0, 2)
     ends = []
     for p, (a1, a2, a3) in enumerate(ORDERS):
         for par in (0, 1):
@@ -320,8 +319,8 @@
                 gt_out[:, pl.ds(p * third, third)] = total
     for i in range(2):
         finish(i)
+    image_block(2, 2)
     for i in range(2, pieces):
-        image_block(i)
         finish(i)
     for p, e, cp in ends:
         cp.wait_recv()

time: 74.2 us -> 75 us (1.011)
  Pallas kernels: 69.2 us -> 70.1 us
    pallas_call x1, Pallas kernels: 69.2 us -> 70.1 us  [shards(): pl.pallas_call(functools.partial(kernel, 2), out_shape=(pltpu.VMEM((rows,...]
where the time goes in v6:
time: 75 us; the launch traced here: 74.9 us
  Pallas kernels  70.1 us (93%)
  local copies, waits for them, and re-layouts  2.85 us (4%)
  between operations  1.93 us (3%)
    pallas_call x1, Pallas kernels, shards(): pl.pallas_call(functools.partial(kernel, 2), out_shape=(pltpu.VMEM((rows,...  70.1 us
    unnamed x2, local copies, waits for them, and re-layouts  2.85 us

profile of v6, /device:TPU:0, one launch (start us, length us, event | category | flops | bytes accessed | tf_op | source)
XLA Modules:
  0.0 74.9 jit_solution(14026418465833553922)
XLA Ops:
  1.9 70.1 %shard_map.68 = (f32[1024,1152]{1,0:T(8,128)S(1)}, f32[32,1152]{1,0:T(8,128)S(1)}) custom-call(f32[1,1]{1,0:T(1,128)} %bitcast.3.scale_ref, f32[1,1]{1,0:T(1,128)} %bitcast.4.bias_ref, s32[8,128]{1,0:T(8,128)} %bitcast.5, bf16[1024,1152]{1,0:T(8,128)(2,1)} %images_ref.1, bf16[32,1152]{1,0:T(8,128)(2,1)} %texts_ref.1), custom_call_target="tpu_custom_call" | custom-call | flops 28991029248 | bytes 9437184 | tf_op jit(solution)/shard_map/pallas_call | solution.py:362
  72.0 2.2 %copy.9 = f32[1024,1152]{1,0:T(8,128)} copy(f32[1024,1152]{1,0:T(8,128)S(1)} %get-tuple-element.2) | data formatting | bytes 9437184
  74.2 0.7 copy.10
